TPU v7x, 128 devices: a whole 4x4x4 slice. The times are simulated.
128 devices in a mesh: inst: 4 (over x_hi, core), seq: 32 (over y, z, x_lo).
Axes of the slice: x: 4 (x_hi: 2, x_lo: 2; x = x_hi * 2 + x_lo), y: 4, z: 4, core: 2. Of those that a mesh axis runs over, the one named last changes fastest.
Arguments:
- query_rows: bfloat16 [16384, 8192], P(('inst', 'seq')), may hold values from -25 to 25
- key_rows: bfloat16 [16384, 1024], P(('inst', 'seq')), may hold values from -4 to 4
- value_rows: bfloat16 [16384, 1024], P(('inst', 'seq')), may hold values from -6 to 6
- target_instance: int32 [8192], P(('inst', 'seq')), may hold values from 0 to 3, as said below
- block_position: int32 [8192], P(('inst', 'seq')), may hold values from 0 to 2047, as said below
- request_lengths: int32 [4, 2], replicated, may hold values from 1 to 3584, 4096 in all within a row
Outputs:
- attended: bfloat16 [16384, 8192], P(('inst', 'seq'))
Inputs may be any that keep to these rules, and one draw needn't show every extreme that they name: `target_instance`: together with block_position, every pair of an instance and a position block is named by exactly one entry block. Of the 64 blocks of one entry device, at most 1 name one instance and block positions b (values of block_position) with the same b // 64, and at most 1 name one instance and block positions with the same min(h, 63 - h), where h = b // 32; both bounds are reached. `block_position`: see target_instance.
All inputs are finite; a program needn't handle non-finite values.
Results may differ from a plain program's by a relative error of at most 0.0055.
Values may be sent and summed in bfloat16 or wider, within the bound.
No kernel may reach another device: no remote copies, remote signals or barrier semaphores. Data moves between devices by JAX's collectives and lax.ppermute only.
A program may use at most 128 MiB of HBM per device.

v0:
```python
import math

import jax
import jax.numpy as jnp
from jax import lax
from jax.sharding import PartitionSpec as P

QUERY_HEADS = 64
KEY_HEADS = 8
HEAD_SIZE = 128


def layout_position(global_rows, row_count, block_rows, half_blocks):
    shard_of = global_rows // row_count
    local_rows = global_rows % row_count
    local_block = local_rows // block_rows
    within = local_rows % block_rows
    offset = local_block % half_blocks
    upper = local_block // half_blocks
    halves = 2 * shard_of + upper
    return (halves * half_blocks + offset) * block_rows + within


def shards(query_rows, key_rows, value_rows, target_instance, block_position, request_lengths):
    inst_count = lax.axis_size("inst")
    seq_count = lax.axis_size("seq")
    devices = inst_count * seq_count
    blocks = block_position.shape[0]
    row_count = query_rows.shape[0]
    block_rows = row_count // blocks
    half_blocks = blocks // 2
    capacity = blocks // (2 * seq_count)
    groups = QUERY_HEADS // KEY_HEADS
    query_width = query_rows.shape[1]
    key_width = key_rows.shape[1]
    score_scale = 1.0 / math.sqrt(HEAD_SIZE)
    own_shard = lax.axis_index("seq")
    instance = lax.axis_index("inst")
    halves = block_position // half_blocks
    offset = block_position % half_blocks
    owner_shard = halves // 2
    local_block = halves % 2 * half_blocks + offset
    target = target_instance * seq_count + owner_shard
    ordinal = jnp.arange(blocks)
    before = (target[:, None] == target[None, :]) & (ordinal[None, :] < ordinal[:, None])
    slot_index = jnp.sum(before.astype(jnp.int32), axis=1)
    destination = target * capacity + slot_index

    def pack_rows(payload, width):
        empty = jnp.zeros((devices * capacity, block_rows, width), payload.dtype)
        filled = empty.at[destination].set(payload.reshape(blocks, block_rows, width))
        return filled.reshape(inst_count, seq_count, capacity, block_rows, width)

    send_query = pack_rows(query_rows, query_width)
    send_key = pack_rows(key_rows, key_width)
    send_value = pack_rows(value_rows, key_width)
    labels = (
        jnp.full((devices * capacity,), -1.0, jnp.bfloat16)
        .at[destination]
        .set(local_block.astype(jnp.bfloat16))
    )
    labels = labels.reshape(inst_count, seq_count, capacity)
    got_query, got_key, got_value, got_label = (
        lax.all_to_all(
            send_query.reshape(devices, capacity, block_rows, query_width),
            ("inst", "seq"),
            split_axis=0,
            concat_axis=0,
            tiled=True,
        ),
        lax.all_to_all(
            send_key.reshape(devices, capacity, block_rows, key_width),
            ("inst", "seq"),
            split_axis=0,
            concat_axis=0,
            tiled=True,
        ),
        lax.all_to_all(
            send_value.reshape(devices, capacity, block_rows, key_width),
            ("inst", "seq"),
            split_axis=0,
            concat_axis=0,
            tiled=True,
        ),
        lax.all_to_all(
            labels.reshape(devices, capacity),
            ("inst", "seq"),
            split_axis=0,
            concat_axis=0,
            tiled=True,
        ),
    )
    received = got_label.reshape(-1).astype(jnp.int32)
    placed = jnp.where(received < 0, blocks, received)

    def unpack_rows(payload, width):
        empty = jnp.zeros((blocks, block_rows, width), payload.dtype)
        filled = empty.at[placed].set(payload.reshape(-1, block_rows, width), mode="drop")
        return filled.reshape(row_count, width)

    local_query = unpack_rows(got_query, query_width)
    local_key = unpack_rows(got_key, key_width)
    local_value = unpack_rows(got_value, key_width)
    lengths_here = lax.dynamic_index_in_dim(request_lengths, instance, 0, keepdims=False)
    request_ends = jnp.cumsum(lengths_here)
    query_pos = layout_position(
        own_shard * row_count + jnp.arange(row_count), row_count, block_rows, half_blocks
    )
    query_start = jnp.sum(
        jnp.where(request_ends[None, :] <= query_pos[:, None], lengths_here[None, :], 0), axis=1
    )
    query_heads = local_query.reshape(row_count, KEY_HEADS, groups, HEAD_SIZE)

    def attend(running, key_block, value_block, key_index):
        key_pos = layout_position(key_index, row_count, block_rows, half_blocks)
        allowed = (key_pos[None, :] <= query_pos[:, None]) & (
            key_pos[None, :] >= query_start[:, None]
        )
        maxima, totals, weighted = running
        key_heads = key_block.reshape(-1, KEY_HEADS, HEAD_SIZE)
        value_heads = value_block.reshape(-1, KEY_HEADS, HEAD_SIZE)
        scores = (
            jnp.einsum("qhgd,khd->hgqk", query_heads, key_heads, preferred_element_type=jnp.float32)
            * score_scale
        )
        masked = jnp.where(allowed, scores, -1e30)
        new_maxima = jnp.maximum(maxima, jnp.max(masked, axis=-1))
        weights = jnp.where(allowed, jnp.exp(scores - new_maxima[..., None]), 0.0)
        rescale = jnp.exp(maxima - new_maxima)
        totals = totals * rescale + jnp.sum(weights, axis=-1)
        weighted = weighted * rescale[..., None] + jnp.einsum(
            "hgqk,khd->hgqd",
            weights.astype(jnp.bfloat16),
            value_heads,
            preferred_element_type=jnp.float32,
        )
        return (new_maxima, totals, weighted)

    initial = (
        jnp.full((KEY_HEADS, groups, row_count), -1e30, jnp.float32),
        jnp.zeros((KEY_HEADS, groups, row_count), jnp.float32),
        jnp.zeros((KEY_HEADS, groups, row_count, HEAD_SIZE), jnp.float32),
    )
    running = initial
    key_piece = lax.all_gather(local_key, "seq", axis=0, tiled=True)
    value_piece = lax.all_gather(local_value, "seq", axis=0, tiled=True)
    piece_rows = key_piece.shape[0]
    shard_count = piece_rows // row_count
    keyed = key_piece.reshape(shard_count, row_count, key_width)
    valued = value_piece.reshape(shard_count, row_count, key_width)
    offsets = jnp.arange(shard_count) * row_count

    def scan_step(state, element):
        key_block, value_block, first_row = element
        return (attend(state, key_block, value_block, first_row + jnp.arange(row_count)), None)

    running, unused = lax.scan(scan_step, running, (keyed, valued, offsets))
    maxima, totals, weighted = running
    attended_local = (
        (weighted / totals[..., None])
        .transpose(2, 0, 1, 3)
        .reshape(row_count, query_width)
        .astype(jnp.bfloat16)
    )
    out_blocks = attended_local.reshape(blocks, block_rows, query_width)
    returning = out_blocks[jnp.clip(received, 0, blocks - 1)]
    returned = lax.all_to_all(
        returning.reshape(devices, capacity, block_rows, query_width),
        ("inst", "seq"),
        split_axis=0,
        concat_axis=0,
        tiled=True,
    )
    gathered_back = returned.reshape(devices * capacity, block_rows, query_width)[destination]
    return gathered_back.reshape(row_count, query_width)


def solution(mesh):
    placed = (
        P(("inst", "seq"), None),
        P(("inst", "seq"), None),
        P(("inst", "seq"), None),
        P(("inst", "seq")),
        P(("inst", "seq")),
        P(),
    )
    return jax.shard_map(
        shards, mesh=mesh, in_specs=placed, out_specs=P(("inst", "seq"), None), check_vma=False
    )
```

profile of v0, /device:TPU:1, one launch (start us, length us, event | category | flops | bytes accessed | tf_op | source)
XLA Modules:
  0.0 1056.4 jit_solution(14671933270696867781)
XLA Ops:
  9.8 11.5 %all-to-all-start = ((bf16[128,1,1]{2,1,0:T(2,128)(2,1)}), bf16[128,1,1]{2,1,0:T(2,128)(2,1)S(1)}, u32[]{:S(2)}, u32[]{:S(2)}) async-start(bf16[128,1,1]{2,1,0:T(2,128)(2,1)} %copy.43), calls=%async_computation | async-start | bytes 131072 | tf_op jit(solution)/shard_map/all_to_all | solution.py:85
  23.5 7.9 scatter_fusion.4
  31.4 9.8 all-to-all-start.3
  43.6 11.3 %all-to-all-done.3 = bf16[128,1,2,1024]{3,2,1,0:T(2,128)(2,1)S(1)} async-done(((bf16[128,1,2,1024]{3,2,1,0:T(2,128)(2,1)}), bf16[128,1,2,1024]{3,2,1,0:T(2,128)(2,1)S(1)}, u32[]{:S(2)}, u32[]{:S(2)}) %all-to-all-start.3) | async-done | bytes 524320 | tf_op jit(solution)/shard_map/all_to_all | solution.py:78
  63.2 23.9 %all_to_all.29 = bf16[128,1,2,1024]{3,2,1,0:T(2,128)(2,1)S(1)} all-to-all(bf16[128,1,2,1024]{3,2,1,0:T(2,128)(2,1)S(1)} %bitcast.80), channel_id=1, replica_groups=mesh['inst'=4,'seq'=32] {'inst','seq'}, dimensions={0} | all-to-all | bytes 1048576 | tf_op jit(solution)/shard_map/all_to_all | solution.py:71
  95.8 6.2 broadcast_in_dim.95
  101.9 14.7 %scatter_fusion.2 = bf16[128,2,8192]{2,1,0:T(2,128)(2,1)} fusion(bf16[128,2,8192]{2,1,0:T(2,128)(2,1)} %broadcast_in_dim.95, s32[64]{0:T(128)S(1)} %compare_select_fusion.21, bf16[64,2,8192]{2,1,0:T(2,128)(2,1)S(1)} %reshape.356), kind=kCustom, calls=%fused_computation.5 | custom fusion | bytes 6291712 | tf_op jit(solution)/shard_map/scatter | solution.py:51
  122.9 99.8 %all-to-all-done.2 = bf16[128,1,2,8192]{3,2,1,0:T(2,128)(2,1)} async-done(((bf16[128,1,2,8192]{3,2,1,0:T(2,128)(2,1)}), bf16[128,1,2,8192]{3,2,1,0:T(2,128)(2,1)}, u32[]{:S(2)}, u32[]{:S(2)}) %all-to-all-start.2) | async-done | bytes 4194336 | tf_op jit(solution)/shard_map/all_to_all | solution.py:64
  224.8 20.7 %scatter_fusion.3 = bf16[64,2,8192]{2,1,0:T(2,128)(2,1)S(1)} fusion(bf16[64,2,8192]{2,1,0:T(2,128)(2,1)S(1)} %broadcast_in_dim.94, s32[128]{0:T(128)S(1)} %get-tuple-element.300, bf16[128,2,8192]{2,1,0:T(2,128)(2,1)} %bitcast.7), kind=kCustom, calls=%fused_computation.6 | custom fusion | bytes 12583424 | tf_op jit(solution)/shard_map/scatter | solution.py:98
  251.2 44.3 %all-gather.5.cloned.1.call-done = bf16[4096,1024]{1,0:T(8,128)(2,1)} async-done(((bf16[128,1024]{1,0:T(8,128)(2,1)}), bf16[4096,1024]{1,0:T(8,128)(2,1)}) %all-gather.5.cloned.1.call-update) | async-done | bytes 8388624 | tf_op jit(solution)/shard_map/all_gather | solution.py:146
  295.5 193.8 %all-gather.3.cloned.1.call-done = bf16[4096,1024]{1,0:T(8,128)(2,1)} async-done(((bf16[128,1024]{1,0:T(8,128)(2,1)}), bf16[4096,1024]{1,0:T(8,128)(2,1)}) %all-gather.3.cloned.1.call-update) | async-done | bytes 8388624 | tf_op jit(solution)/shard_map/all_gather | solution.py:145
  489.3 470.0 %while.18 = (s32[]{:T(128)}, f32[8,8,128]{2,1,0:T(8,128)S(1)}, f32[8,8,128]{2,1,0:T(8,128)S(1)}, f32[8,8,128,128]{3,2,1,0:T(8,128)}, s32[32]{0:T(128)S(1)}, /*in...) while((s32[]{:T(128)}, f32[8,8,128]{2,1,0:T(8,128)S(1)}, ...), condition=%wide.region_13.14_spmd.clone, body=%wide.region_10.13_spmd.clone.sunk | while | flops 551657472 | bytes 26282648 | solution.py:157
  512.1 5.9 fusion.52
  526.8 5.9 fusion.52
  570.9 5.9 fusion.52
  585.7 5.9 fusion.52
  600.4 5.9 fusion.52
  615.1 5.9 fusion.52
  629.8 5.9 fusion.52
  673.9 5.9 fusion.52
  718.1 5.9 fusion.52
  732.8 5.9 fusion.52
  747.5 5.9 fusion.52
  776.9 5.9 fusion.52
  791.6 5.9 fusion.52
  821.0 5.9 fusion.52
  835.8 5.9 fusion.52
  850.5 5.9 fusion.52
  967.4 11.8 %gather_fusion = bf16[128,2,8192]{2,1,0:T(2,128)(2,1)} fusion(bf16[64,2,8192]{2,1,0:T(2,128)(2,1)S(1)} %convert_element_type.46, s32[1024]{0:T(1024)S(1)} %pad_clamp_fusion.1), kind=kCustom, calls=%fused_computation | custom fusion | bytes 8389120 | tf_op jit(solution)/shard_map/gather | solution.py:166
  979.2 6.6 all-to-all-start.4
  985.8 53.2 %all-to-all-done.4 = bf16[128,1,2,8192]{3,2,1,0:T(2,128)(2,1)} async-done(((bf16[128,1,2,8192]{3,2,1,0:T(2,128)(2,1)}), bf16[128,1,2,8192]{3,2,1,0:T(2,128)(2,1)}, u32[]{:S(2)}, u32[]{:S(2)}) %all-to-all-start.4) | async-done | bytes 4194336 | tf_op jit(solution)/shard_map/all_to_all | solution.py:167
  1039.0 8.4 gather_fusion.1
  (417 shorter events, 423.8 us)
Async XLA Ops:
  6.5 115.9 %copy-start = (s32[4,2]{0,1:T(2,128)S(1)}, s32[4,2]{0,1:T(2,128)}, u32[]{:S(2)}) copy-start(s32[4,2]{0,1:T(2,128)} %param.13) | copy-start | bytes 100
  6.5 53.9 %copy-start.2 = (bf16[128,1024]{1,0:T(8,128)(2,1)S(1)}, bf16[128,1024]{1,0:T(8,128)(2,1)}, u32[]{:S(2)}) copy-start(bf16[128,1024]{1,0:T(8,128)(2,1)} %param.9) | copy-start | bytes 786436
  9.8 21.5 %all-to-all-start = ((bf16[128,1,1]{2,1,0:T(2,128)(2,1)}), bf16[128,1,1]{2,1,0:T(2,128)(2,1)S(1)}, u32[]{:S(2)}, u32[]{:S(2)}) async-start(bf16[128,1,1]{2,1,0:T(2,128)(2,1)} %copy.43), calls=%async_computation | async-start | bytes 131072 | tf_op jit(solution)/shard_map/all_to_all | solution.py:85
  31.4 23.5 %all-to-all-start.3 = ((bf16[128,1,2,1024]{3,2,1,0:T(2,128)(2,1)}), bf16[128,1,2,1024]{3,2,1,0:T(2,128)(2,1)S(1)}, u32[]{:S(2)}, u32[]{:S(2)}) async-start(bf16[128,1,2,1024]{3,2,1,0:T(2,128)(2,1)} %bitcast.9), calls=%async_computation.3 | async-start | bytes 1048576 | tf_op jit(solution)/shard_map/all_to_all | solution.py:78
  41.1 254.4 %all-gather.5.cloned.1.call-start = ((), (), s32[]{:S(2)}) async-start(), calls=%async_computation.6 | async-start | bytes 8650752 | tf_op jit(solution)/shard_map/all_gather | solution.py:146
  60.3 429.0 %all-gather.3.cloned.1.call-start = ((), (), s32[]{:S(2)}) async-start(), calls=%async_computation.5 | async-start | bytes 8650752 | tf_op jit(solution)/shard_map/all_gather | solution.py:145
  116.6 106.1 %all-to-all-start.2 = ((bf16[128,1,2,8192]{3,2,1,0:T(2,128)(2,1)}), bf16[128,1,2,8192]{3,2,1,0:T(2,128)(2,1)}, u32[]{:S(2)}, u32[]{:S(2)}) async-start(bf16[128,1,2,8192]{3,2,1,0:T(2,128)(2,1)} %bitcast.78), calls=%async_computation.2 | async-start | bytes 8388608 | tf_op jit(solution)/shard_map/all_to_all | solution.py:64
  979.2 59.8 %all-to-all-start.4 = ((bf16[128,1,2,8192]{3,2,1,0:T(2,128)(2,1)}), bf16[128,1,2,8192]{3,2,1,0:T(2,128)(2,1)}, u32[]{:S(2)}, u32[]{:S(2)}) async-start(bf16[128,1,2,8192]{3,2,1,0:T(2,128)(2,1)} %bitcast.79), calls=%async_computation.4 | async-start | bytes 8388608 | tf_op jit(solution)/shard_map/all_to_all | solution.py:167
  1039.0 10.6 %copy-start.1 = (s32[4,2]{0,1:T(2,128)S(1)}, s32[4,2]{0,1:T(2,128)}, u32[]{:S(2)}) copy-start(s32[4,2]{0,1:T(2,128)} %param.13) | copy-start | bytes 100
Sparse Core Ops, SparseCore 0:
  60.5 235.0 all-gather.4
  297.2 192.0 all-gather.2
where the time goes:
time: 1060 us
  waiting for transfers between devices  402 us (38%)
  matrix products  277 us (26%)
  local copies, waits for them, and re-layouts  169 us (16%)
  other arithmetic  135 us (13%)
  starting transfers between devices  33.7 us (3%)
  blocking collectives  23.9 us (2%)
  between operations  13.6 us (1%)
    all_gather x1, waiting for transfers between devices, shards(): key_piece = lax.all_gather(local_key, 'seq', axis=0, tiled=True)  194 us
    dot_general x32, matrix products, attend(): jnp.einsum('hgqk,khd->hgqd', weights.astype(jnp.bfloat16), value_heads, p...  187 us
    reduce_sum x32, other arithmetic, attend(): totals = totals * rescale + jnp.sum(weights, axis=-1)  103 us
    all_to_all x1, waiting for transfers between devices, shards(): lax.all_to_all(send_query.reshape(devices, capacity, block_rows, query_wi...  99.8 us
    dot_general x32, matrix products, attend(): jnp.einsum('qhgd,khd->hgqk', query_heads, key_heads, preferred_element_ty...  90 us
    dynamic_slice x128, local copies, waits for them, and re-layouts, shards(): running, unused = lax.scan(scan_step, running, (keyed, valued, offsets))  63.7 us
    all_to_all x1, waiting for transfers between devices, shards(): lax.all_to_all(returning.reshape(devices, capacity, block_rows, query_wid...  53.2 us
    all_gather x1, waiting for transfers between devices, shards(): value_piece = lax.all_gather(local_value, 'seq', axis=0, tiled=True)  44.3 us
  transfers between devices with their start and end apart: 6, of which 5 were waited for; matrix products, arithmetic and copies ran while one was open for 7% of the time, Pallas kernels for 0%

commit v1 on v0

v1 whole, which is shorter than its diff:
```python
import functools
import math

import jax
import jax.numpy as jnp
from jax import lax
from jax.experimental import pallas as pl
from jax.experimental.pallas import tpu as pltpu
from jax.sharding import PartitionSpec as P

BOTH = ("inst", "seq")
INSTANCES = 4
DEVICES = 128
KEY_HEADS = 8
HEAD = 128
BLOCKS = 64
ROWS = 128
CAP = 16
SLOTS = INSTANCES * CAP
SEQ_BLOCKS = 2048
POSITIONS = 4096
TILE = 256
TILES = SEQ_BLOCKS // TILE
SENT = 6 * CAP
CHUNK = SENT + 8
BACK = 4 * CAP
LOG2E = math.log2(math.e)
F32 = jnp.float32
BF16 = jnp.bfloat16


def ranks(plan):
    shape = (ROWS, ROWS)
    inst_l = jnp.broadcast_to(plan[0:1, :].astype(F32), shape)
    pos_l = jnp.broadcast_to(plan[1:2, :].astype(F32), shape)
    inst_s, pos_s = inst_l.T, pos_l.T
    lane = lax.broadcasted_iota(jnp.int32, shape, 1)
    sub = lax.broadcasted_iota(jnp.int32, shape, 0)
    same = inst_l == inst_s
    rank_l = jnp.sum(
        jnp.where(same & (pos_s < pos_l) & (sub % 2 == 0), 1.0, 0.0), axis=0, keepdims=True
    )
    rank_s = jnp.sum(
        jnp.where(same & (pos_l < pos_s) & (lane % 2 == 0), 1.0, 0.0), axis=1, keepdims=True
    )
    return inst_l, pos_l, inst_s, pos_s, rank_l, rank_s, lane, sub


def pack_kernel(first, plan_ref, q_ref, k_ref, v_ref, out_ref, pick_ref, label_ref):
    @pl.when(pl.program_id(0) == 0)
    def _():
        inst_l, _, inst_s, pos_s, rank_l, rank_s, lane, sub = ranks(plan_ref[...])
        turn = rank_l - first
        slot = jnp.where((turn >= 0) & (turn < CAP), inst_l[0:1] * CAP + turn, -1.0)
        hit = (jnp.broadcast_to(slot, (SLOTS, ROWS)) == sub[:SLOTS].astype(F32))
        for parity in range(2):
            pick_ref[parity] = jnp.where(hit & (lane[:SLOTS] % 2 == parity), 1.0, 0.0).astype(BF16)
        most = jnp.broadcast_to(jnp.max(rank_l, axis=1, keepdims=True) + 1.0, (8, ROWS))
        row = sub[:8]
        for i in range(INSTANCES):
            here = (inst_s == i) & (rank_s == lane.astype(F32)) & (sub % 2 == 0)
            block = jnp.sum(jnp.where(here, pos_s + 1.0, 0.0), axis=0, keepdims=True) - 1.0
            high = jnp.floor(block * (1.0 / 64.0))
            low = block - high * 64.0
            label = jnp.where(
                row == 0, jnp.broadcast_to(high, (8, ROWS)), jnp.broadcast_to(low, (8, ROWS))
            )
            label_ref[i] = jnp.where(row < 2, label, jnp.where(row == 2, most, 0.0)).astype(BF16)

    for parity in range(2):
        pick = pick_ref[parity]
        queries = jnp.dot(pick, q_ref[...], preferred_element_type=F32).astype(BF16)
        keys = jnp.dot(pick, k_ref[...], preferred_element_type=F32).astype(BF16)
        values = jnp.dot(pick, v_ref[...], preferred_element_type=F32).astype(BF16)
        for i in range(INSTANCES):
            rows = slice(i * CAP, (i + 1) * CAP)
            for r in range(4):
                to = (i // 2, r % 2, i % 2, 0, r // 2)
                for h in range(2):
                    at = (2 * parity + h) * CAP
                    head = (2 * r + h) * HEAD
                    out_ref[(*to, slice(at, at + CAP), slice(None))] = queries[rows, head : head + HEAD]
                if r % 2 == parity:
                    out_ref[(*to, slice(4 * CAP, 5 * CAP), slice(None))] = keys[rows]
                    out_ref[(*to, slice(5 * CAP, 6 * CAP), slice(None))] = values[rows]
                if parity == 0:
                    out_ref[(*to, slice(SENT, CHUNK), slice(None))] = label_ref[i]


def pack(turn, plan, q, k, v):
    group = 8 * HEAD
    return pl.pallas_call(
        functools.partial(pack_kernel, turn * CAP),
        grid=(KEY_HEADS,),
        in_specs=[
            pl.BlockSpec((2, ROWS), lambda g: (0, 0)),
            pl.BlockSpec((ROWS, group), lambda g: (0, g)),
            pl.BlockSpec((ROWS, HEAD), lambda g: (0, g)),
            pl.BlockSpec((ROWS, HEAD), lambda g: (0, g)),
        ],
        out_specs=pl.BlockSpec((2, 2, 2, 1, 2, CHUNK, HEAD), lambda g: (0, 0, 0, g, 0, 0, 0)),
        out_shape=jax.ShapeDtypeStruct((2, 2, 2, KEY_HEADS, 2, CHUNK, HEAD), BF16),
        scratch_shapes=[pltpu.VMEM((2, SLOTS, ROWS), BF16), pltpu.VMEM((INSTANCES, 8, ROWS), BF16)],
        name="pack",
    )(plan, q, k, v).reshape(DEVICES, CHUNK, HEAD)


def sort_kernel(parts, pos_ref, rows_ref, out_ref):
    slots = pos_ref.shape[1]
    wanted = lax.broadcasted_iota(jnp.int32, (TILE, slots), 0) + pl.program_id(0) * TILE
    pick = jnp.where(pos_ref[...] == wanted, 1.0, 0.0).astype(BF16)
    for c in range(0, parts, 2):
        pair = [rows_ref[:, p * CAP : (p + 1) * CAP, :].reshape(slots, HEAD) for p in (c, c + 1)]
        found = jnp.dot(pick, jnp.concatenate(pair, axis=1), preferred_element_type=F32).astype(BF16)
        out_ref[c] = found[:, :HEAD]
        out_ref[c + 1] = found[:, HEAD:]


def sort_rows(name, first, parts, pos_row, rows):
    slots = pos_row.shape[1]
    return pl.pallas_call(
        functools.partial(sort_kernel, parts),
        grid=(TILES,),
        in_specs=[
            pl.BlockSpec((1, slots), lambda t: (0, 0)),
            pl.BlockSpec((rows.shape[0], parts * CAP, HEAD), lambda t: (0, first // parts, 0)),
        ],
        out_specs=pl.BlockSpec((parts, TILE, HEAD), lambda t: (0, t, 0)),
        out_shape=jax.ShapeDtypeStruct((parts, SEQ_BLOCKS, HEAD), BF16),
        compiler_params=pltpu.CompilerParams(vmem_limit_bytes=40 << 20),
        cost_estimate=pl.CostEstimate(
            flops=2 * SEQ_BLOCKS * slots * parts * HEAD, bytes_accessed=4 << 20, transcendentals=0
        ),
        name=name,
    )(pos_row, rows)


def attend_kernel(facts_ref, q_ref, own_ref, other_ref, out_ref, top_ref, sum_ref):
    tile = pl.program_id(0)
    core = facts_ref[0]
    span = 2 * TILE
    queries = q_ref[...].reshape(4 * TILE, HEAD)
    scale = LOG2E / math.sqrt(HEAD)

    def start_of(position):
        start, end = jnp.int32(0), jnp.int32(0)
        for d in range(1, facts_ref.shape[0]):
            end = end + facts_ref[d]
            start = jnp.where(end <= position, end, start)
        return start

    def step(at, masked, fresh):
        keys_at = pl.ds(pl.multiple_of(at * TILE, TILE), TILE)
        keys = jnp.concatenate([own_ref[0, keys_at, :], other_ref[0, keys_at, :]], axis=0)
        values = jnp.concatenate([own_ref[1, keys_at, :], other_ref[1, keys_at, :]], axis=0)
        values = jnp.concatenate([values, jnp.ones((span, HEAD), BF16)], axis=1)
        scores = lax.dot_general(
            queries, keys, (((1,), (1,)), ((), ())), preferred_element_type=F32
        )
        if masked:
            row = lax.broadcasted_iota(jnp.int32, (4 * TILE, 1), 0)
            query_pos = tile * span + (row % TILE) * 2 + row // (2 * TILE)
            start, end = jnp.zeros_like(query_pos), jnp.int32(0)
            for d in range(1, facts_ref.shape[0]):
                end = end + facts_ref[d]
                start = jnp.where(end <= query_pos, end, start)
            lane = lax.broadcasted_iota(jnp.int32, (1, span), 1)
            parity = jnp.where(lane < TILE, core, 1 - core)
            key_pos = at * span + (lane % TILE) * 2 + parity
            scores = jnp.where((key_pos <= query_pos) & (key_pos >= start), scores, -1e30)
        best = jnp.max(scores, axis=1, keepdims=True) * scale
        if fresh:
            top = jnp.broadcast_to(best, (4 * TILE, HEAD))
        else:
            before = top_ref[...]
            top = jnp.maximum(before, best)
        weights = jnp.exp2(scores * scale - jnp.concatenate([top] * (span // HEAD), axis=1))
        added = jnp.dot(weights.astype(BF16), values, preferred_element_type=F32)
        if fresh:
            sum_ref[...] = added
        else:
            keep = jnp.exp2(before - top)
            sum_ref[...] = sum_ref[...] * jnp.concatenate([keep, keep], axis=1) + added
        top_ref[...] = top

    step(tile, True, True)
    low = start_of(tile * span) // span
    clear = jnp.clip((start_of(tile * span + span - 1) + span - 1) // span, low, tile)

    @pl.loop(low, clear)
    def _(at):
        step(at, True, False)

    @pl.loop(clear, tile)
    def _(at):
        step(at, False, False)

    done = sum_ref[:, :HEAD] / sum_ref[:, HEAD:]
    out_ref[...] = done.astype(BF16).reshape(4, TILE, HEAD)


def attend(facts, queries, own, other):
    return pl.pallas_call(
        attend_kernel,
        grid=(TILES,),
        in_specs=[
            pl.BlockSpec(memory_space=pltpu.SMEM),
            pl.BlockSpec((4, TILE, HEAD), lambda t: (0, t, 0)),
            pl.BlockSpec((2, SEQ_BLOCKS, HEAD), lambda t: (0, 0, 0)),
            pl.BlockSpec((2, SEQ_BLOCKS, HEAD), lambda t: (0, 0, 0)),
        ],
        out_specs=pl.BlockSpec((4, TILE, HEAD), lambda t: (0, t, 0)),
        out_shape=jax.ShapeDtypeStruct((4, SEQ_BLOCKS, HEAD), BF16),
        scratch_shapes=[
            pltpu.VMEM((4 * TILE, HEAD), F32),
            pltpu.VMEM((4 * TILE, 2 * HEAD), F32),
        ],
        compiler_params=pltpu.CompilerParams(vmem_limit_bytes=48 << 20),
        name="attend",
    )(facts, queries, own, other)


def unsort_kernel(pos_ref, rows_ref, out_ref):
    block = lax.broadcasted_iota(jnp.int32, (TILE, SEQ_BLOCKS), 1)
    pick = jnp.where(pos_ref[...] == block, 1.0, 0.0).astype(BF16)
    for c in range(0, 4, 2):
        pair = jnp.concatenate([rows_ref[c], rows_ref[c + 1]], axis=1)
        found = jnp.dot(pick, pair, preferred_element_type=F32).astype(BF16)
        for p in range(2):
            part = found[:, p * HEAD : (p + 1) * HEAD].reshape(TILE // CAP, CAP, HEAD)
            out_ref[:, (c + p) * CAP : (c + p + 1) * CAP, :] = part


def unsort_rows(pos_column, rows):
    slots = pos_column.shape[0]
    return pl.pallas_call(
        unsort_kernel,
        grid=(slots // TILE,),
        in_specs=[
            pl.BlockSpec((TILE, 1), lambda t: (t, 0)),
            pl.BlockSpec((4, SEQ_BLOCKS, HEAD), lambda t: (0, 0, 0)),
        ],
        out_specs=pl.BlockSpec((TILE // CAP, BACK, HEAD), lambda t: (t, 0, 0)),
        out_shape=jax.ShapeDtypeStruct((slots // CAP, BACK, HEAD), BF16),
        compiler_params=pltpu.CompilerParams(vmem_limit_bytes=40 << 20),
        name="unsort",
    )(pos_column, rows)


def unpack_kernel(rounds, plan_ref, *refs):
    back_refs, out_ref, place_ref = refs[:rounds], refs[rounds], refs[rounds + 1]

    @pl.when(pl.program_id(0) == 0)
    def _():
        _, _, inst_s, _, _, rank_s, lane, sub = ranks(plan_ref[...])
        for turn in range(rounds):
            step = rank_s - turn * CAP
            slot = jnp.where((step >= 0) & (step < CAP), inst_s[:, :SLOTS] * CAP + step, -1.0)
            hit = slot == lane[:, :SLOTS].astype(F32)
            for parity in range(2):
                place_ref[turn, parity] = jnp.where(
                    hit & (sub[:, :SLOTS] % 2 == parity), 1.0, 0.0
                ).astype(BF16)

    total = jnp.zeros(out_ref.shape, F32)
    for turn in range(rounds):
        for parity in range(2):
            lines = []
            for i in range(INSTANCES):
                line = []
                for r in range(4):
                    of = (i // 2, r % 2, i % 2, 0, r // 2)
                    for h in range(2):
                        at = (2 * parity + h) * CAP
                        line.append(back_refs[turn][(*of, slice(at, at + CAP), slice(None))])
                lines.append(jnp.concatenate(line, axis=1))
            total = total + jnp.dot(
                place_ref[turn, parity], jnp.concatenate(lines, axis=0), preferred_element_type=F32
            )
    out_ref[...] = total.astype(BF16)


def unpack(plan, backs):
    group = 8 * HEAD
    rounds = len(backs)
    return pl.pallas_call(
        functools.partial(unpack_kernel, rounds),
        grid=(KEY_HEADS,),
        in_specs=[pl.BlockSpec((2, ROWS), lambda g: (0, 0))]
        + [pl.BlockSpec((2, 2, 2, 1, 2, BACK, HEAD), lambda g: (0, 0, 0, g, 0, 0, 0))] * rounds,
        out_specs=pl.BlockSpec((ROWS, group), lambda g: (0, g)),
        out_shape=jax.ShapeDtypeStruct((ROWS, KEY_HEADS * group), BF16),
        scratch_shapes=[pltpu.VMEM((rounds, 2, ROWS, SLOTS), BF16)],
        name="unpack",
    )(plan, *(b.reshape(2, 2, 2, KEY_HEADS, 2, BACK, HEAD) for b in backs))


def exchange(x):
    return lax.all_to_all(x, BOTH, split_axis=0, concat_axis=0, tiled=True)


def shards(query_rows, key_rows, value_rows, target_instance, block_position, request_lengths):
    spot = lax.axis_index("inst")
    core = spot % 2
    instance = (spot // 2) * 2 + lax.axis_index("seq") // 16
    plan = jnp.repeat(jnp.stack([target_instance, block_position]), 2, axis=1)
    lengths = lax.dynamic_index_in_dim(request_lengths, instance, 0, keepdims=False)
    facts = jnp.concatenate([core[None], lengths]).astype(jnp.int32)

    got = exchange(pack(0, plan, query_rows, key_rows, value_rows))
    labels = got[:, SENT : SENT + 3, : 2 * CAP].astype(jnp.int32)
    positions = labels[:, 0] * 64 + labels[:, 1]
    most = jnp.max(labels[:, 2, 0])

    def finish(rounds):
        rows, where = got, positions[:, :CAP].reshape(-1)
        if rounds == 2:
            more = exchange(pack(1, plan, query_rows, key_rows, value_rows))
            rows = jnp.concatenate([rows, more], axis=0)
            where = jnp.concatenate([where, positions[:, CAP:].reshape(-1)])
        pos_row, pos_column = where[None, :], where[:, None]
        own = sort_rows("sort_keys", 4, 2, pos_row, rows)
        other = lax.ppermute(own, "inst", [(0, 1), (1, 0), (2, 3), (3, 2)])
        queries = sort_rows("sort_queries", 0, 4, pos_row, rows)
        sorted_out = attend(facts, queries, own, other)
        back = unsort_rows(pos_column, sorted_out)
        backs = [exchange(back[t * DEVICES : (t + 1) * DEVICES]) for t in range(rounds)]
        return unpack(plan, backs)

    return lax.cond(most > CAP, lambda: finish(2), lambda: finish(1))


def solution(mesh):
    rows = P(BOTH, None)
    return jax.shard_map(
        shards,
        mesh=mesh,
        in_specs=(rows, rows, rows, P(BOTH), P(BOTH), P()),
        out_specs=rows,
        check_vma=False,
    )
```

time: 1060 us -> 170 us (0.16)
  waiting for transfers between devices: 402 us -> 44.3 us
  matrix products: 277 us -> 0 us
  local copies, waits for them, and re-layouts: 169 us -> 5.4 us
  other arithmetic: 135 us -> 1.68 us
  Pallas kernels: 0 us -> 70.4 us
  starting transfers between devices: 33.7 us -> 12.7 us
  between operations: 13.6 us -> 0.74 us
    dot_general x64 -> x0, matrix products: 277 us -> none  [the longest x32 187 us: attend(): jnp.einsum('hgqk,khd->hgqd', weights.astype(jnp.bfloat16), value_heads, p...]
    all_gather x2 -> x0, waiting for transfers between devices: 238 us -> none  [the longest x1 194 us: shards(): key_piece = lax.all_gather(local_key, 'seq', axis=0, tiled=True)]
    all_to_all x4 -> x1, waiting for transfers between devices: 164 us -> 44.3 us  [exchange(): return lax.all_to_all(x, BOTH, split_axis=0, concat_axis=0, tiled=True)]
    reduce_sum x34 -> x0, other arithmetic: 103 us -> none  [the longest x32 103 us: attend(): totals = totals * rescale + jnp.sum(weights, axis=-1)]
    pallas_call x0 -> x6, Pallas kernels: none -> 70.4 us  [the longest x1 39.3 us: attend(): pl.pallas_call(attend_kernel, grid=(TILES,), in_specs=[pl.BlockSpec(memor...]
    dynamic_slice x128 -> x0, local copies, waits for them, and re-layouts: 63.7 us -> none  [shards(): running, unused = lax.scan(scan_step, running, (keyed, valued, offsets))]
    scatter x7 -> x0, local copies, waits for them, and re-layouts: 55.6 us -> none  [the longest x3 29.6 us: unpack_rows(): empty.at[placed].set(payload.reshape(-1, block_rows, width), mode='drop')]
    add x66 -> x1, other arithmetic: 23 us -> 0.08 us  [shards(): positions = labels[:, 0] * 64 + labels[:, 1]]
  transfers between devices with their start and end apart: 6 -> 2, of which waited for: 5 -> 1; matrix products, arithmetic and copies ran while one was open for 7% -> 0% of each run, Pallas kernels for 0% -> 4%
where the time goes in v1:
time: 170 us
  Pallas kernels  70.4 us (41%)
  waiting for transfers between devices  44.3 us (26%)
  blocking collectives  34.2 us (20%)
  starting transfers between devices  12.7 us (7%)
  local copies, waits for them, and re-layouts  5.4 us (3%)
    all_to_all x1, waiting for transfers between devices, exchange(): return lax.all_to_all(x, BOTH, split_axis=0, concat_axis=0, tiled=True)  44.3 us
    pallas_call x1, Pallas kernels, attend(): pl.pallas_call(attend_kernel, grid=(TILES,), in_specs=[pl.BlockSpec(memor...  39.3 us
    all_to_all x1, blocking collectives, exchange(): return lax.all_to_all(x, BOTH, split_axis=0, concat_axis=0, tiled=True)  34.2 us
    pallas_call x2, Pallas kernels, sort_rows(): pl.pallas_call(functools.partial(sort_kernel, parts), grid=(TILES,), in_s...  12.5 us
    all_to_all x1, starting transfers between devices, exchange(): return lax.all_to_all(x, BOTH, split_axis=0, concat_axis=0, tiled=True)  11.5 us
    pallas_call x1, Pallas kernels, pack(): pl.pallas_call(functools.partial(pack_kernel, turn * CAP), grid=(KEY_HEAD...  7.05 us
    pallas_call x1, Pallas kernels, unsort_rows(): pl.pallas_call(unsort_kernel, grid=(slots // TILE,), in_specs=[pl.BlockSp...  6.06 us
    pallas_call x1, Pallas kernels, unpack(): pl.pallas_call(functools.partial(unpack_kernel, rounds), grid=(KEY_HEADS,...  5.52 us
  transfers between devices with their start and end apart: 2, of which 1 were waited for; matrix products, arithmetic and copies ran while one was open for 0% of the time, Pallas kernels for 4%

profile of v1, /device:TPU:1, one launch (start us, length us, event | category | flops | bytes accessed | tf_op | source)
XLA Modules:
  0.0 169.8 jit_solution(5777628283667370291)
XLA Ops:
  0.0 0.0 copy-start
  0.0 0.7 pad_add_fusion
  0.7 0.1 broadcast_in_dim.12
  0.8 0.1 reshape.33.plan_ref
  0.9 7.1 %pack.3 = bf16[2,2,2,8,2,104,128]{6,5,4,3,2,1,0:T(8,128)(2,1)} custom-call(s32[2,128]{1,0:T(2,128)S(1)} %reshape.33.plan_ref, bf16[128,8192]{1,0:T(8,128)(2,1)} %q_ref.1, bf16[128,1024]{1,0:T(8,128)(2,1)} %k_ref.1, bf16[128,1024]{1,0:T(8,128)(2,1)} %v_ref.1), custom_call_target="tpu_custom_call" | custom-call | tf_op jit(solution)/shard_map/pack/pallas_call | solution.py:92
  8.0 11.5 %all-to-all-start.4 = ((bf16[128,104,128]{2,1,0:T(8,128)(2,1)}), bf16[128,104,128]{2,1,0:T(8,128)(2,1)S(1)}, u32[]{:S(2)}, u32[]{:S(2)}) async-start(bf16[128,104,128]{2,1,0:T(8,128)(2,1)} %bitcast.15), calls=%async_computation.4 | async-start | bytes 6815744 | tf_op jit(solution)/shard_map/all_to_all | solution.py:299
  19.5 0.0 copy-done
  19.5 0.2 dynamic-slice_reduce_fusion
  19.7 0.1 pad_add_fusion.1
  19.8 44.3 %all-to-all-done.4 = bf16[128,104,128]{2,1,0:T(8,128)(2,1)S(1)} async-done(((bf16[128,104,128]{2,1,0:T(8,128)(2,1)}), bf16[128,104,128]{2,1,0:T(8,128)(2,1)S(1)}, u32[]{:S(2)}, u32[]{:S(2)}) %all-to-all-start.4) | async-done | bytes 3407904 | tf_op jit(solution)/shard_map/all_to_all | solution.py:299
  64.1 0.1 slice_convert_fusion
  64.2 0.1 slice_add_fusion
  64.3 0.8 slice_reduce_fusion
  65.7 102.8 %conditional.1 = (bf16[128,8192]{1,0:T(8,128)(2,1)S(1)}) conditional(s32[]{:T(128)} %convert_element_type.7, (s32[128,32]{1,0:T(8,128)S(1)}, bf16[128,104,128]{2,1,0:T(8,128)(2,1)S(1)}, s32[3]{0:T(128)S(1)}, s32[2,128]{1,0:T(2,128)S(1)}) %tuple.20, (s32[128,32]{1,0:T(8,128)S(1)}, s32[2,128]{1,0:T(2,128)S(1)}, bf16[128,8192]{1,0:T(8,128)(2,1)}, ...), branch_computations={%region_1.2_spmd, %region_2.3_spmd} | conditional | flops 12884901888 | bytes 129892552 | solution.py:330
  65.7 0.0 copy-start.5
  65.7 1.7 %copy-done.5 = bf16[128,104,128]{2,1,0:T(8,128)(2,1)} copy-done((bf16[128,104,128]{2,1,0:T(8,128)(2,1)}, bf16[128,104,128]{2,1,0:T(8,128)(2,1)S(1)}, u32[]{:S(2)}) %copy-start.5) | copy-done | bytes 3407896 | tf_op jit(solution)/shard_map/cond
  67.4 0.1 reshape.24.pos_ref
  67.5 5.0 %sort_keys.2.own_ref = bf16[2,2048,128]{2,1,0:T(8,128)(2,1)S(1)} custom-call(s32[1,2048]{1,0:T(1,128)S(1)} %reshape.24.pos_ref, bf16[128,104,128]{2,1,0:T(8,128)(2,1)} %copy-done.5), custom_call_target="tpu_custom_call" | custom-call | flops 2147483648 | bytes 4194304 | tf_op jit(solution)/shard_map/cond/branch_0_fun/sort_keys/pallas_call | solution.py:121
  72.5 1.2 collective-permute-start
  73.7 0.6 reshape.35.pos_ref
  74.3 7.5 %sort_queries.2.q_ref = bf16[4,2048,128]{2,1,0:T(8,128)(2,1)S(1)} custom-call(s32[1,2048]{1,0:T(1,128)S(1)} %reshape.24.pos_ref, bf16[128,104,128]{2,1,0:T(8,128)(2,1)} %copy-done.5), custom_call_target="tpu_custom_call" | custom-call | flops 4294967296 | bytes 4194304 | tf_op jit(solution)/shard_map/cond/branch_0_fun/sort_queries/pallas_call | solution.py:121
  81.8 0.0 copy-start.2
  81.8 1.3 copy-done.2
  83.1 0.0 collective-permute-done.other_ref
  83.1 39.3 %attend.2.rows_ref = bf16[4,2048,128]{2,1,0:T(8,128)(2,1)S(1)} custom-call(s32[3]{0:T(128)S(1)} %get-tuple-element.32.facts_ref, bf16[4,2048,128]{2,1,0:T(8,128)(2,1)} %copy-done.2, bf16[2,2048,128]{2,1,0:T(8,128)(2,1)S(1)} %sort_keys.2.own_ref, bf16[2,2048,128]{2,1,0:T(8,128)(2,1)S(1)} %collective-permute-done.other_ref), custom_call_target="tpu_custom_call" | custom-call | tf_op jit(solution)/shard_map/cond/branch_0_fun/attend/pallas_call | solution.py:203
  122.5 6.1 %unsort.2 = bf16[128,64,128]{2,1,0:T(8,128)(2,1)S(1)} custom-call(s32[2048,1]{1,0:T(8,128)S(1)} %reshape.35.pos_ref, bf16[4,2048,128]{2,1,0:T(8,128)(2,1)S(1)} %attend.2.rows_ref), custom_call_target="tpu_custom_call" | custom-call | tf_op jit(solution)/shard_map/cond/branch_0_fun/unsort/pallas_call | solution.py:236
  128.5 34.2 %all_to_all.21 = bf16[128,64,128]{2,1,0:T(8,128)(2,1)} all-to-all(bf16[128,64,128]{2,1,0:T(8,128)(2,1)S(1)} %unsort.2), channel_id=1, replica_groups=mesh['inst'=4,'seq'=32] {'inst','seq'}, dimensions={0} | all-to-all | bytes 4194304 | tf_op jit(solution)/shard_map/cond/branch_0_fun/all_to_all | solution.py:299
  162.8 5.5 %unpack.2 = bf16[128,8192]{1,0:T(8,128)(2,1)S(1)} custom-call(s32[2,128]{1,0:T(2,128)S(1)} %get-tuple-element.30.plan_ref, bf16[2,2,2,8,2,64,128]{6,5,4,3,2,1,0:T(8,128)(2,1)} %bitcast.17), custom_call_target="tpu_custom_call" | custom-call | tf_op jit(solution)/shard_map/cond/branch_0_fun/unpack/pallas_call | solution.py:286
  168.5 0.0 copy-start.7
  168.5 1.3 copy-done.7
Async XLA Ops:
  0.0 19.5 %copy-start = (s32[4,2]{0,1:T(2,128)S(1)}, s32[4,2]{0,1:T(2,128)}, u32[]{:S(2)}) copy-start(s32[4,2]{0,1:T(2,128)} %param.13) | copy-start | bytes 100
  8.0 56.2 %all-to-all-start.4 = ((bf16[128,104,128]{2,1,0:T(8,128)(2,1)}), bf16[128,104,128]{2,1,0:T(8,128)(2,1)S(1)}, u32[]{:S(2)}, u32[]{:S(2)}) async-start(bf16[128,104,128]{2,1,0:T(8,128)(2,1)} %bitcast.15), calls=%async_computation.4 | async-start | bytes 6815744 | tf_op jit(solution)/shard_map/all_to_all | solution.py:299
  65.7 1.7 %copy-start.5 = (bf16[128,104,128]{2,1,0:T(8,128)(2,1)}, bf16[128,104,128]{2,1,0:T(8,128)(2,1)S(1)}, u32[]{:S(2)}) copy-start(bf16[128,104,128]{2,1,0:T(8,128)(2,1)S(1)} %get-tuple-element.33.rows_ref) | copy-start | bytes 10223620 | tf_op jit(solution)/shard_map/cond
  72.5 10.6 %collective-permute-start = (bf16[2,2048,128]{2,1,0:T(8,128)(2,1)S(1)}, bf16[2,2048,128]{2,1,0:T(8,128)(2,1)S(1)}, u32[]{:S(2)}, u32[]{:S(2)}) collective-permute-start(bf16[2,2048,128]{2,1,0:T(8,128)(2,1)S(1)} %sort_keys.2.own_ref), channel_id=1, source_target_pairs={{0,32},{32,0},{64,96},{96,64},{1,33},{33,1},{65,97},{97,65},{2,34}... | collective-permute-start | bytes 3145736 | tf_op jit(solution)/shard_map/cond/branch_0_fun/ppermute | solution.py:323
  81.8 1.3 copy-start.2
  168.5 1.3 copy-start.7

commit v2 on v1

v2 whole, which is shorter than its diff:
```python
import functools
import math

import jax
import jax.numpy as jnp
from jax import lax
from jax.experimental import pallas as pl
from jax.experimental.pallas import tpu as pltpu
from jax.sharding import PartitionSpec as P

BOTH = ("inst", "seq")
INSTANCES = 4
DEVICES = 128
KEY_HEADS = 8
HEAD = 128
ROWS = 128
CAP = 16
SLOTS = INSTANCES * CAP
SEQ_BLOCKS = 2048
TILE = 256
TILES = SEQ_BLOCKS // TILE
SORTED = 512
SENT = 6 * CAP
CHUNK = SENT + 8
BACK = 4 * CAP
GROUP = 2
WIDE = GROUP * 8 * HEAD
SCALE = math.log2(math.e) / math.sqrt(HEAD)
ROOM = pltpu.CompilerParams(vmem_limit_bytes=58 << 20)
F32 = jnp.float32
BF16 = jnp.bfloat16


def ranks(facts_ref):
    shape = (ROWS, ROWS)
    inst_l = jnp.broadcast_to(facts_ref[0:1, :].astype(F32), shape)
    pos_l = jnp.broadcast_to(facts_ref[1:2, :].astype(F32), shape)
    inst_s, pos_s = inst_l.T, pos_l.T
    lane = lax.broadcasted_iota(jnp.int32, shape, 1)
    sub = lax.broadcasted_iota(jnp.int32, shape, 0)
    same = inst_l == inst_s
    rank_l = jnp.sum(
        jnp.where(same & (pos_s < pos_l) & (sub % 2 == 0), 1.0, 0.0), axis=0, keepdims=True
    )
    rank_s = jnp.sum(
        jnp.where(same & (pos_l < pos_s) & (lane % 2 == 0), 1.0, 0.0), axis=1, keepdims=True
    )
    return inst_l, inst_s, pos_s, rank_l, rank_s, lane, sub


def pack_kernel(turn, plan_ref, q_ref, k_ref, v_ref, out_ref, pick_ref, label_ref):
    @pl.when(pl.program_id(0) == 0)
    def _():
        inst_l, inst_s, pos_s, rank_l, rank_s, lane, sub = ranks(plan_ref)
        step = rank_l - turn * CAP
        slot = jnp.where((step >= 0) & (step < CAP), inst_l[0:1] * CAP + step, -1.0)
        hit = (slot == (sub % SLOTS).astype(F32)) & (lane % 2 == sub // SLOTS)
        pick_ref[...] = jnp.where(hit, 1.0, 0.0).astype(BF16)
        most = jnp.max(rank_l, axis=1, keepdims=True) + 1.0
        row = sub[:8]
        place = lane - plan_ref[2:3, :]
        for i in range(INSTANCES):
            label = jnp.where(row == 4, most, 0.0)
            for t in range(2):
                here = (inst_s == i) & (rank_s == (place + t * CAP).astype(F32))
                here = here & (place >= 0) & (place < CAP) & (sub % 2 == 0)
                block = jnp.sum(jnp.where(here, pos_s + 1.0, 0.0), axis=0, keepdims=True)
                high = jnp.floor(block * (1.0 / 64.0))
                label = jnp.where(row == 2 * t, high, label)
                label = jnp.where(row == 2 * t + 1, block - high * 64.0, label)
            label_ref[i] = label.astype(BF16)

    pick = pick_ref[...]
    queries = jnp.dot(pick, q_ref[...], preferred_element_type=F32).astype(BF16)
    keys = jnp.dot(pick, k_ref[...], preferred_element_type=F32).astype(BF16)
    values = jnp.dot(pick, v_ref[...], preferred_element_type=F32).astype(BF16)
    for i in range(INSTANCES):
        for g in range(GROUP):
            for r in range(4):
                to = (i // 2, r % 2, i % 2, g, r // 2)
                for c in range(4):
                    at = (c // 2) * SLOTS + i * CAP
                    head = (8 * g + 2 * r + c % 2) * HEAD
                    out_ref[(*to, slice(c * CAP, (c + 1) * CAP), slice(None))] = queries[
                        at : at + CAP, head : head + HEAD
                    ]
                at = (r % 2) * SLOTS + i * CAP
                lanes = slice(g * HEAD, (g + 1) * HEAD)
                out_ref[(*to, slice(4 * CAP, 5 * CAP), slice(None))] = keys[at : at + CAP, lanes]
                out_ref[(*to, slice(5 * CAP, 6 * CAP), slice(None))] = values[at : at + CAP, lanes]
                out_ref[(*to, slice(SENT, CHUNK), slice(None))] = label_ref[i]


def pack(turn, plan, q, k, v):
    return pl.pallas_call(
        functools.partial(pack_kernel, turn),
        grid=(KEY_HEADS // GROUP,),
        in_specs=[
            pl.BlockSpec((3, ROWS), lambda g: (0, 0)),
            pl.BlockSpec((ROWS, WIDE), lambda g: (0, g)),
            pl.BlockSpec((ROWS, GROUP * HEAD), lambda g: (0, g)),
            pl.BlockSpec((ROWS, GROUP * HEAD), lambda g: (0, g)),
        ],
        out_specs=pl.BlockSpec((2, 2, 2, GROUP, 2, CHUNK, HEAD), lambda g: (0, 0, 0, g, 0, 0, 0)),
        out_shape=jax.ShapeDtypeStruct((2, 2, 2, KEY_HEADS, 2, CHUNK, HEAD), BF16),
        scratch_shapes=[pltpu.VMEM((ROWS, ROWS), BF16), pltpu.VMEM((INSTANCES, 8, ROWS), BF16)],
        compiler_params=ROOM,
        name="pack",
    )(plan, q, k, v).reshape(DEVICES, CHUNK, HEAD)


def slot_positions(turn, rows_ref):
    label = rows_ref[:, SENT:CHUNK, :].astype(F32).reshape(DEVICES // 8, 8, 8, HEAD)
    label = jnp.sum(label, axis=1)
    row = lax.broadcasted_iota(jnp.int32, label.shape, 1)
    part = jnp.where(row == 2 * turn, label * 64.0, jnp.where(row == 2 * turn + 1, label, 0.0))
    return jnp.sum(part, axis=1) - 1.0


def line_up(pos):
    return jnp.concatenate([pos[j : j + 1] for j in range(DEVICES // 8)], axis=1)


def sorted_pair(line_ref, rows_refs, c):
    slots = DEVICES * CAP
    wanted = lax.broadcasted_iota(jnp.int32, (SORTED, slots), 0) + pl.program_id(0) * SORTED
    found = None
    for turn, rows_ref in enumerate(rows_refs):
        pick = jnp.where(line_ref[turn, 0:1, :] == wanted, 1.0, 0.0).astype(BF16)
        pair = [rows_ref[:, p * CAP : (p + 1) * CAP, :].reshape(slots, HEAD) for p in (c, c + 1)]
        added = jnp.dot(pick, jnp.concatenate(pair, axis=1), preferred_element_type=F32)
        found = added if found is None else found + added
    return found


def sort_keys_kernel(rounds, *refs):
    rows_refs = refs[:rounds]
    keys_ref, values_ref, line_ref, column_ref, most_ref = refs[rounds:]

    @pl.when(pl.program_id(0) == 0)
    def _():
        for turn in range(rounds):
            pos = slot_positions(turn, rows_refs[0])
            line_ref[turn] = jnp.broadcast_to(line_up(pos).astype(jnp.int32), (8, DEVICES * CAP))
            empty = jnp.zeros((HEAD - DEVICES // 8, HEAD), F32)
            column_ref[turn] = jnp.concatenate([pos, empty], axis=0).T
        count = rows_refs[0][:, SENT:CHUNK, :].astype(F32)
        row = lax.broadcasted_iota(jnp.int32, count.shape, 1)
        most_ref[0] = jnp.max(jnp.where(row == 4, count, 0.0)).astype(jnp.int32)

    found = sorted_pair(line_ref, rows_refs, 4)
    keys_ref[...] = found[:, :HEAD].astype(BF16)
    values_ref[...] = found[:, HEAD:].T.astype(BF16)


def sort_keys(rows):
    rounds, slots = len(rows), DEVICES * CAP
    line, column = (rounds, 8, slots), (rounds, HEAD, HEAD)
    return pl.pallas_call(
        functools.partial(sort_keys_kernel, rounds),
        grid=(SEQ_BLOCKS // SORTED,),
        in_specs=[pl.BlockSpec((DEVICES, CHUNK, HEAD), lambda t: (0, 0, 0))] * rounds,
        out_specs=(
            pl.BlockSpec((SORTED, HEAD), lambda t: (t, 0)),
            pl.BlockSpec((HEAD, SORTED), lambda t: (0, t)),
            pl.BlockSpec(line, lambda t: (0, 0, 0)),
            pl.BlockSpec(column, lambda t: (0, 0, 0)),
            pl.BlockSpec(memory_space=pltpu.SMEM),
        ),
        out_shape=(
            jax.ShapeDtypeStruct((SEQ_BLOCKS, HEAD), BF16),
            jax.ShapeDtypeStruct((HEAD, SEQ_BLOCKS), BF16),
            jax.ShapeDtypeStruct(line, jnp.int32),
            jax.ShapeDtypeStruct(column, F32),
            jax.ShapeDtypeStruct((1,), jnp.int32),
        ),
        compiler_params=ROOM,
        name="sort_keys",
    )(*rows)


def sort_queries_kernel(line_ref, *refs):
    out_ref = refs[-1]
    for c in range(0, 4, 2):
        found = sorted_pair(line_ref, refs[:-1], c).astype(BF16)
        out_ref[c] = found[:, :HEAD]
        out_ref[c + 1] = found[:, HEAD:]


def sort_queries(line, rows):
    flops = 2 * SEQ_BLOCKS * DEVICES * CAP * len(rows) * 4 * HEAD
    return pl.pallas_call(
        sort_queries_kernel,
        grid=(SEQ_BLOCKS // SORTED,),
        in_specs=[pl.BlockSpec(line.shape, lambda t: (0, 0, 0))]
        + [pl.BlockSpec((DEVICES, 4 * CAP, HEAD), lambda t: (0, 0, 0))] * len(rows),
        out_specs=pl.BlockSpec((4, SORTED, HEAD), lambda t: (0, t, 0)),
        out_shape=jax.ShapeDtypeStruct((4, SEQ_BLOCKS, HEAD), BF16),
        compiler_params=ROOM,
        cost_estimate=pl.CostEstimate(flops=flops, bytes_accessed=4 << 20, transcendentals=0),
        name="sort_queries",
    )(line, *rows)


def attend_tile(
    tile, facts_ref, q_ref, own_keys, own_values, other_keys, other_values, out_ref, sum_ref, top_ref
):
    core = facts_ref[0]
    span = 2 * TILE
    columns = 4 * TILE
    first = tile * span

    def start_of(position):
        start, end = jnp.zeros_like(position), jnp.int32(0)
        for d in range(1, facts_ref.shape[0]):
            end = end + facts_ref[d]
            start = jnp.where(end <= position, end, start)
        return start

    column = lax.broadcasted_iota(jnp.int32, (1, columns), 1)
    query_pos = first + (column % TILE) * 2 + column // (2 * TILE)
    query_start = start_of(query_pos)

    def key_pos(at, index):
        own = index < TILE
        block = jnp.where(own, index, index - TILE) + at * TILE
        return block * 2 + jnp.where(own, core, 1 - core)

    def scores_of(at, wide):
        at_keys = pl.ds(pl.multiple_of(at * TILE, TILE), wide * TILE)
        keys = jnp.concatenate([own_keys[at_keys, :], other_keys[at_keys, :]], axis=0)
        scores = lax.dot_general(
            keys,
            q_ref[...].reshape(columns, HEAD),
            (((1,), (1,)), ((), ())),
            preferred_element_type=F32,
        )
        return scores * SCALE

    def allowed(at, whole):
        pos = key_pos(at, lax.broadcasted_iota(jnp.int32, (span, 1), 0))
        return (pos <= query_pos) & (pos >= query_start) if whole else pos <= query_pos

    def mixed(at, wide, weights, start=None):
        at_keys = pl.ds(pl.multiple_of(at * TILE, TILE), wide * TILE)
        values = jnp.concatenate([own_values[:, at_keys], other_values[:, at_keys]], axis=1)
        ones = jnp.ones((16, wide * span), BF16)
        if start is not None:
            pos = key_pos(at, lax.broadcasted_iota(jnp.int32, (16, span), 1))
            ones = jnp.where(pos >= start, 1.0, 0.0).astype(BF16)
            values = values * ones[0:1]
        values = jnp.concatenate([values, ones], axis=0)
        return jnp.dot(values, weights.astype(BF16), preferred_element_type=F32)

    start = start_of(first)
    low = start // span
    clear = jnp.minimum((start + span - 1) // span, tile)
    split = start_of(first + span - 1) > first

    def plain(at, wide, start=None):
        sum_ref[...] += mixed(at, wide, jnp.exp2(scores_of(at, wide)), start)

    sum_ref[...] = jnp.zeros_like(sum_ref)

    @pl.when(low < clear)
    def _():
        plain(low, 1, start)

    left = tile - clear
    for wide in (1, 2, 4):

        @pl.when((left // wide) % 2 == 1)
        def _():
            plain(clear + left % wide, wide)

    def diagonal(whole):
        weights = jnp.exp2(jnp.where(allowed(tile, whole), scores_of(tile, 1), -1e30))
        added = mixed(tile, 1, weights)
        if whole:
            sum_ref[...] = jnp.where(query_start <= first, sum_ref[...], 0.0) + added
        else:
            sum_ref[...] += added

    @pl.when(split)
    def _():
        diagonal(True)

    @pl.when(jnp.logical_not(split))
    def _():
        diagonal(False)

    total = sum_ref[HEAD : HEAD + 8]
    fine = (jnp.max(total) <= 2.0**100) & (jnp.min(total) >= 2.0**-80)

    @pl.when(jnp.logical_not(fine))
    def _():
        def shifted(at, begins):
            scores = jnp.where(allowed(at, True), scores_of(at, 1), -1e30)
            best = jnp.broadcast_to(jnp.max(scores, axis=0, keepdims=True), (8, columns))
            top = best if begins else jnp.maximum(top_ref[...], best)
            added = mixed(at, 1, jnp.exp2(scores - top[0:1]))
            if begins:
                sum_ref[...] = added
            else:
                sum_ref[...] = sum_ref[...] * jnp.exp2(top_ref[0:1] - top[0:1]) + added
            top_ref[...] = top

        shifted(tile, True)

        @pl.loop(low, tile)
        def _(at):
            shifted(at, False)

    done = (sum_ref[:HEAD] / sum_ref[HEAD : HEAD + 1]).astype(BF16)
    place = pl.ds(pl.multiple_of(tile * TILE, TILE), TILE)
    for c in range(4):
        out_ref[c * HEAD : (c + 1) * HEAD, place] = done[:, c * TILE : (c + 1) * TILE]


def unsort_tile(tile, column_ref, attended_ref, out_ref):
    lane = lax.broadcasted_iota(jnp.int32, (HEAD, HEAD), 1)
    turn, near = tile // TILES, tile % TILES
    columns = [
        jnp.sum(jnp.where(lane == near * 2 + j, column_ref[turn], 0.0), axis=1, keepdims=True)
        for j in range(2)
    ]
    pos = jnp.concatenate(columns, axis=0).astype(jnp.int32)
    block = lax.broadcasted_iota(jnp.int32, (TILE, SEQ_BLOCKS), 1)
    pick = jnp.where(pos == block, 1.0, 0.0).astype(BF16)
    for c in range(0, 4, 2):
        found = lax.dot_general(
            pick,
            attended_ref[c * HEAD : (c + 2) * HEAD, :],
            (((1,), (1,)), ((), ())),
            preferred_element_type=F32,
        ).astype(BF16)
        for p in range(2):
            part = found[:, p * HEAD : (p + 1) * HEAD].reshape(TILE // CAP, CAP, HEAD)
            out_ref[:, (c + p) * CAP : (c + p + 1) * CAP, :] = part


def attend_kernel(facts_ref, column_ref, q_ref, *refs):
    key_refs, out_ref, attended_ref, more = refs[:4], refs[4], refs[5], refs[6:]
    step = pl.program_id(0)

    @pl.when(step < TILES)
    def _():
        attend_tile(step, facts_ref, q_ref, *key_refs, attended_ref, *more)

    @pl.when(step >= TILES)
    def _():
        unsort_tile(step - TILES, column_ref, attended_ref, out_ref)


def attend(facts, column, queries, own, other):
    rounds = column.shape[0]
    keys = pl.BlockSpec((SEQ_BLOCKS, HEAD), lambda t: (0, 0))
    values = pl.BlockSpec((HEAD, SEQ_BLOCKS), lambda t: (0, 0))
    return pl.pallas_call(
        attend_kernel,
        grid=(TILES + rounds * TILES,),
        in_specs=[
            pl.BlockSpec(memory_space=pltpu.SMEM),
            pl.BlockSpec(column.shape, lambda t: (0, 0, 0)),
            pl.BlockSpec((4, TILE, HEAD), lambda t: (0, jnp.minimum(t, TILES - 1), 0)),
            keys,
            values,
            keys,
            values,
        ],
        out_specs=pl.BlockSpec(
            (DEVICES // TILES, BACK, HEAD), lambda t: (jnp.maximum(t - TILES, 0), 0, 0)
        ),
        out_shape=jax.ShapeDtypeStruct((rounds * DEVICES, BACK, HEAD), BF16),
        scratch_shapes=[
            pltpu.VMEM((4 * HEAD, SEQ_BLOCKS), BF16),
            pltpu.VMEM((HEAD + 16, 4 * TILE), F32),
            pltpu.VMEM((8, 4 * TILE), F32),
        ],
        compiler_params=ROOM,
        name="attend",
    )(facts, column, queries, *own, *other)


def unpack_kernel(rounds, plan_ref, *refs):
    back_refs, out_ref, place_ref = refs[:rounds], refs[rounds], refs[rounds + 1]

    @pl.when(pl.program_id(0) == 0)
    def _():
        _, inst_s, _, _, rank_s, lane, sub = ranks(plan_ref)
        for turn in range(rounds):
            step = rank_s - turn * CAP
            slot = jnp.where((step >= 0) & (step < CAP), inst_s * CAP + step, -1.0)
            hit = (slot == (lane % SLOTS).astype(F32)) & (sub % 2 == lane // SLOTS)
            place_ref[turn] = jnp.where(hit, 1.0, 0.0).astype(BF16)

    total = jnp.zeros(out_ref.shape, F32)
    for turn in range(rounds):
        lines = []
        for parity in range(2):
            for i in range(INSTANCES):
                line = []
                for g in range(GROUP):
                    for r in range(4):
                        of = (i // 2, r % 2, i % 2, g, r // 2)
                        for h in range(2):
                            at = (2 * parity + h) * CAP
                            line.append(back_refs[turn][(*of, slice(at, at + CAP), slice(None))])
                lines.append(jnp.concatenate(line, axis=1))
        total = total + jnp.dot(
            place_ref[turn], jnp.concatenate(lines, axis=0), preferred_element_type=F32
        )
    out_ref[...] = total.astype(BF16)


def unpack(plan, backs):
    rounds = len(backs)
    block = pl.BlockSpec((2, 2, 2, GROUP, 2, BACK, HEAD), lambda g: (0, 0, 0, g, 0, 0, 0))
    return pl.pallas_call(
        functools.partial(unpack_kernel, rounds),
        grid=(KEY_HEADS // GROUP,),
        in_specs=[pl.BlockSpec((3, ROWS), lambda g: (0, 0))] + [block] * rounds,
        out_specs=pl.BlockSpec((ROWS, WIDE), lambda g: (0, g)),
        out_shape=jax.ShapeDtypeStruct((ROWS, KEY_HEADS * 8 * HEAD), BF16),
        scratch_shapes=[pltpu.VMEM((rounds, ROWS, ROWS), BF16)],
        compiler_params=ROOM,
        name="unpack",
    )(plan, *(b.reshape(2, 2, 2, KEY_HEADS, 2, BACK, HEAD) for b in backs))


def exchange(x):
    return lax.all_to_all(x, BOTH, split_axis=0, concat_axis=0, tiled=True)


def shards(query_rows, key_rows, value_rows, target_instance, block_position, request_lengths):
    spot, place = lax.axis_index("inst"), lax.axis_index("seq")
    core = spot % 2
    instance = (spot // 2) * 2 + place // 16
    offset = jnp.full_like(block_position, (place % 8) * CAP)
    plan = jnp.repeat(jnp.stack([target_instance, block_position, offset]), 2, axis=1)
    lengths = lax.dynamic_index_in_dim(request_lengths, instance, 0, keepdims=False)
    facts = jnp.concatenate([core[None], lengths]).astype(jnp.int32)

    def run(rounds):
        rows = [exchange(pack(t, plan, query_rows, key_rows, value_rows)) for t in range(rounds)]
        keys, values, line, column, most = sort_keys(rows)
        pairs = [(0, 1), (1, 0), (2, 3), (3, 2)]
        other = [lax.ppermute(x, "inst", pairs) for x in (keys, values)]
        back = attend(facts, column, sort_queries(line, rows), (keys, values), other)
        backs = [exchange(back[t * DEVICES : (t + 1) * DEVICES]) for t in range(rounds)]
        return unpack(plan, backs), most[0]

    attended, most = run(1)
    return lax.while_loop(
        lambda state: state[1] > CAP,
        lambda state: (run(2)[0], jnp.zeros_like(state[1])),
        (attended, most),
    )[0]


def solution(mesh):
    rows = P(BOTH, None)
    return jax.shard_map(
        shards,
        mesh=mesh,
        in_specs=(rows, rows, rows, P(BOTH), P(BOTH), P()),
        out_specs=rows,
        check_vma=False,
    )
```

time: 170 us -> 184 us (1.082)
  blocking collectives: 34.2 us -> 91.9 us
  waiting for transfers between devices: 44.3 us -> 0.01 us
  Pallas kernels: 70.4 us -> 87.3 us
  starting transfers between devices: 12.7 us -> 1.18 us
  local copies, waits for them, and re-layouts: 5.4 us -> 2.05 us
    all_to_all x1 -> x2, blocking collectives: 34.2 us -> 91.9 us  [exchange(): return lax.all_to_all(x, BOTH, split_axis=0, concat_axis=0, tiled=True)]
    all_to_all x1 -> x0, waiting for transfers between devices: 44.3 us -> none  [exchange(): return lax.all_to_all(x, BOTH, split_axis=0, concat_axis=0, tiled=True)]
    pallas_call x6 -> x5, Pallas kernels: 70.4 us -> 87.3 us  [the longest x1 64 us: attend(): pl.pallas_call(attend_kernel, grid=(TILES + rounds * TILES,), in_specs=[p...]
    all_to_all x1 -> x0, starting transfers between devices: 11.5 us -> none  [exchange(): return lax.all_to_all(x, BOTH, split_axis=0, concat_axis=0, tiled=True)]
    cond x4 -> x0, local copies, waits for them, and re-layouts: 3.02 us -> none
  transfers between devices with their start and end apart: 2 -> 2, of which waited for: 1 -> 0; matrix products, arithmetic and copies ran while one was open for 0% -> 0% of each run, Pallas kernels for 4% -> 4%
where the time goes in v2:
time: 184 us
  blocking collectives  91.9 us (50%)
  Pallas kernels  87.3 us (47%)
  local copies, waits for them, and re-layouts  2.05 us (1%)
    all_to_all x2, blocking collectives, exchange(): return lax.all_to_all(x, BOTH, split_axis=0, concat_axis=0, tiled=True)  91.9 us
    pallas_call x1, Pallas kernels, attend(): pl.pallas_call(attend_kernel, grid=(TILES + rounds * TILES,), in_specs=[p...  64 us
    pallas_call x1, Pallas kernels, sort_queries(): pl.pallas_call(sort_queries_kernel, grid=(SEQ_BLOCKS // SORTED,), in_spec...  7.51 us
    pallas_call x1, Pallas kernels, sort_keys(): pl.pallas_call(functools.partial(sort_keys_kernel, rounds), grid=(SEQ_BLO...  6.16 us
    pallas_call x1, Pallas kernels, pack(): pl.pallas_call(functools.partial(pack_kernel, turn), grid=(KEY_HEADS // G...  4.99 us
    pallas_call x1, Pallas kernels, unpack(): pl.pallas_call(functools.partial(unpack_kernel, rounds), grid=(KEY_HEADS...  4.62 us
  transfers between devices with their start and end apart: 2, of which 0 were waited for; matrix products, arithmetic and copies ran while one was open for 0% of the time, Pallas kernels for 4%

profile of v2, /device:TPU:1, one launch (start us, length us, event | category | flops | bytes accessed | tf_op | source)
XLA Modules:
  0.0 184.3 jit_solution(10506838214533940017)
XLA Ops:
  0.0 0.0 copy-start
  0.0 0.1 pad.4.clone
  0.1 0.7 add_add_fusion
  0.8 0.1 broadcast_in_dim.6
  0.9 0.7 reshape.21.plan_ref
  1.6 5.0 %pack.3 = bf16[2,2,2,8,2,104,128]{6,5,4,3,2,1,0:T(8,128)(2,1)} custom-call(s32[3,128]{1,0:T(4,128)} %reshape.21.plan_ref, bf16[128,8192]{1,0:T(8,128)(2,1)} %q_ref.1, bf16[128,1024]{1,0:T(8,128)(2,1)} %k_ref.1, bf16[128,1024]{1,0:T(8,128)(2,1)} %v_ref.1), custom_call_target="tpu_custom_call" | custom-call | tf_op jit(solution)/shard_map/pack/pallas_call | solution.py:95
  6.6 56.3 %all_to_all.30.refs_0_ = bf16[128,104,128]{2,1,0:T(8,128)(2,1)} all-to-all(bf16[128,104,128]{2,1,0:T(8,128)(2,1)} %bitcast.15), channel_id=1, replica_groups=mesh['inst'=4,'seq'=32] {'inst','seq'}, dimensions={0} | all-to-all | bytes 6815744 | tf_op jit(solution)/shard_map/all_to_all | solution.py:432
  62.9 6.2 %sort_keys.2 = (bf16[2048,128]{1,0:T(8,128)(2,1)}, bf16[128,2048]{1,0:T(8,128)(2,1)}, s32[1,8,2048]{2,1,0:T(8,128)}, f32[1,128,128]{2,1,0:T(8,128)}, s32[1]{0:T(128)}) custom-call(bf16[128,104,128]{2,1,0:T(8,128)(2,1)} %all_to_all.30.refs_0_), custom_call_target="tpu_custom_call" | custom-call | tf_op jit(solution)/shard_map/sort_keys/pallas_call | solution.py:159
  69.1 1.2 collective-permute-start.2
  70.2 0.0 collective-permute-start.3
  70.2 0.0 copy-done
  70.2 0.2 dynamic-slice_reduce_fusion
  70.4 0.1 pad_add_fusion.facts_ref
  70.5 7.5 %sort_queries.2.q_ref = bf16[4,2048,128]{2,1,0:T(8,128)(2,1)} custom-call(s32[1,8,2048]{2,1,0:T(8,128)} %get-tuple-element.50.line_ref, bf16[128,104,128]{2,1,0:T(8,128)(2,1)} %all_to_all.30.refs_0_), custom_call_target="tpu_custom_call" | custom-call | flops 4294967296 | bytes 4194304 | tf_op jit(solution)/shard_map/sort_queries/pallas_call | solution.py:192
  78.0 0.0 collective-permute-done.2.refs_2_
  78.0 0.0 copy-start.11
  78.0 0.0 collective-permute-done.3.refs_3_
  78.0 0.0 copy-start.12
  78.0 0.8 copy-done.11
  78.8 0.2 copy-done.12
  79.0 64.0 %attend.2 = bf16[128,64,128]{2,1,0:T(8,128)(2,1)} custom-call(s32[3]{0:T(128)S(1)} %pad_add_fusion.facts_ref, f32[1,128,128]{2,1,0:T(8,128)} %get-tuple-element.49.column_ref, bf16[4,2048,128]{2,1,0:T(8,128)(2,1)} %sort_queries.2.q_ref, bf16[2048,128]{1,0:T(8,128)(2,1)} %get-tuple-element.51.refs_0_, bf16[128,2048]{1,0:T(8,128)(2,1)} %get-tuple-element.52.refs_1_, ...), custom_call_target="tpu_custom_call" | custom-call | tf_op jit(solution)/shard_map/attend/pallas_call | solution.py:359
  143.0 35.6 %all_to_all.31 = bf16[128,64,128]{2,1,0:T(8,128)(2,1)} all-to-all(bf16[128,64,128]{2,1,0:T(8,128)(2,1)} %attend.2), channel_id=1, replica_groups=mesh['inst'=4,'seq'=32] {'inst','seq'}, dimensions={0} | all-to-all | bytes 4194304 | tf_op jit(solution)/shard_map/all_to_all | solution.py:432
  178.6 0.0 copy-start.2
  178.6 0.0 copy-start.5
  178.6 0.0 copy-start.7
  178.6 4.6 %unpack.2 = bf16[128,8192]{1,0:T(8,128)(2,1)} custom-call(s32[3,128]{1,0:T(4,128)} %reshape.21.plan_ref, bf16[2,2,2,8,2,64,128]{6,5,4,3,2,1,0:T(8,128)(2,1)} %bitcast.16), custom_call_target="tpu_custom_call" | custom-call | tf_op jit(solution)/shard_map/unpack/pallas_call | solution.py:419
  183.3 0.0 copy-done.2
  183.3 0.0 copy-done.5
  183.3 0.0 copy-done.7
  183.3 0.9 while.10
Async XLA Ops:
  0.0 70.2 %copy-start = (s32[4,2]{0,1:T(2,128)S(1)}, s32[4,2]{0,1:T(2,128)}, u32[]{:S(2)}) copy-start(s32[4,2]{0,1:T(2,128)} %param.13) | copy-start | bytes 100
  69.1 9.0 %collective-permute-start.2 = (bf16[2048,128]{1,0:T(8,128)(2,1)}, bf16[2048,128]{1,0:T(8,128)(2,1)S(1)}, u32[]{:S(2)}, u32[]{:S(2)}) collective-permute-start(bf16[2048,128]{1,0:T(8,128)(2,1)} %get-tuple-element.51.refs_0_), channel_id=1, source_target_pairs={{0,32},{32,0},{64,96},{96,64},{1,33},{33,1},{65,97},{97,65},{2,34}... | collective-permute-start | bytes 1572872 | tf_op jit(solution)/shard_map/ppermute | solution.py:448
  70.2 7.8 %collective-permute-start.3 = (bf16[128,2048]{1,0:T(8,128)(2,1)}, bf16[128,2048]{1,0:T(8,128)(2,1)S(1)}, u32[]{:S(2)}, u32[]{:S(2)}) collective-permute-start(bf16[128,2048]{1,0:T(8,128)(2,1)} %get-tuple-element.52.refs_1_), channel_id=1, source_target_pairs={{0,32},{32,0},{64,96},{96,64},{1,33},{33,1},{65,97},{97,65},{2,34}... | collective-permute-start | bytes 1572872 | tf_op jit(solution)/shard_map/ppermute | solution.py:448
  78.0 0.8 copy-start.11
  78.0 1.0 copy-start.12
  178.6 4.6 %copy-start.2 = (bf16[128,8192]{1,0:T(8,128)(2,1)S(1)}, bf16[128,8192]{1,0:T(8,128)(2,1)}, u32[]{:S(2)}) copy-start(bf16[128,8192]{1,0:T(8,128)(2,1)} %q_ref.1) | copy-start | bytes 6291460
  178.6 4.6 %copy-start.5 = (bf16[128,1024]{1,0:T(8,128)(2,1)S(1)}, bf16[128,1024]{1,0:T(8,128)(2,1)}, u32[]{:S(2)}) copy-start(bf16[128,1024]{1,0:T(8,128)(2,1)} %k_ref.1) | copy-start | bytes 786436
  178.6 4.6 %copy-start.7 = (bf16[128,1024]{1,0:T(8,128)(2,1)S(1)}, bf16[128,1024]{1,0:T(8,128)(2,1)}, u32[]{:S(2)}) copy-start(bf16[128,1024]{1,0:T(8,128)(2,1)} %v_ref.1) | copy-start | bytes 786436

commit v3 on v2

v3 whole, which is shorter than its diff:
```python
import functools
import math

import jax
import jax.numpy as jnp
from jax import lax
from jax.experimental import pallas as pl
from jax.experimental.pallas import tpu as pltpu
from jax.sharding import PartitionSpec as P

BOTH = ("inst", "seq")
INSTANCES = 4
DEVICES = 128
KEY_HEADS = 8
HEAD = 128
ROWS = 128
CAP = 16
SLOTS = INSTANCES * CAP
SEQ_BLOCKS = 2048
TILE = 256
TILES = SEQ_BLOCKS // TILE
SORTED = 1024
TURNS = 2
UNSORTED = 1024
UNSORTS = DEVICES * CAP // UNSORTED
SENT = 6 * CAP
CHUNK = SENT + 8
BACK = 4 * CAP
GROUP = 4
WIDE = GROUP * 8 * HEAD
SCALE = math.log2(math.e) / math.sqrt(HEAD)
ROOM = pltpu.CompilerParams(vmem_limit_bytes=36 << 20)
F32 = jnp.float32
BF16 = jnp.bfloat16


def plan_pack(turn, facts_ref, target_ref, block_ref, pick_ref, label_ref, place_ref):
    shape = (ROWS, ROWS)
    half = jnp.full((1, ROWS // 2), -1.0, F32)
    inst_l = jnp.concatenate([target_ref[...].astype(F32), half], axis=1)
    pos_l = jnp.concatenate([block_ref[...].astype(F32), half], axis=1)
    inst_s, pos_s = jnp.broadcast_to(inst_l, shape).T, jnp.broadcast_to(pos_l, shape).T
    lane = lax.broadcasted_iota(jnp.int32, shape, 1)
    sub = lax.broadcasted_iota(jnp.int32, shape, 0)
    ahead = (inst_l == inst_s) & (pos_l < pos_s)
    rank = jnp.sum(jnp.where(ahead, 1.0, 0.0), axis=1, keepdims=True)
    step = rank - turn * CAP
    slot = jnp.where((step >= 0) & (step < CAP), inst_s * CAP + step, -1.0)
    slot = jnp.sum(jnp.where(lane // 2 == sub, slot, 0.0), axis=0, keepdims=True)
    hit = (slot == (sub % SLOTS).astype(F32)) & (lane % 2 == sub // SLOTS)
    pick = jnp.where(hit, 1.0, 0.0)
    pick_ref[...] = pick.astype(BF16)
    place_ref[...] = pick.T.astype(BF16)
    most = jnp.max(jnp.broadcast_to(rank, shape), axis=0, keepdims=True) + 1.0
    row = sub[:8]
    at = lane - facts_ref[1]
    for i in range(INSTANCES):
        label = jnp.where(row == 4, most, 0.0)
        for t in range(2):
            here = (inst_s == i) & (rank == (at + t * CAP).astype(F32)) & (at >= 0) & (at < CAP)
            block = jnp.sum(jnp.where(here, pos_s + 1.0, 0.0), axis=0, keepdims=True)
            high = jnp.floor(block * (1.0 / 64.0))
            label = jnp.where(row == 2 * t, high, label)
            label = jnp.where(row == 2 * t + 1, block - high * 64.0, label)
        label_ref[i] = label.astype(BF16)


def pack_kernel(turn, facts_ref, target_ref, block_ref, q_ref, k_ref, v_ref, out_ref, place_ref, pick_ref, label_ref):
    @pl.when(pl.program_id(0) == 0)
    def _():
        plan_pack(turn, facts_ref, target_ref, block_ref, pick_ref, label_ref, place_ref)

    pick = pick_ref[...]
    queries = jnp.dot(pick, q_ref[...], preferred_element_type=F32).astype(BF16)
    keys = jnp.dot(pick, k_ref[...], preferred_element_type=F32).astype(BF16)
    values = jnp.dot(pick, v_ref[...], preferred_element_type=F32).astype(BF16)
    for i in range(INSTANCES):
        for g in range(GROUP):
            for r in range(4):
                to = (i // 2, r % 2, i % 2, g, r // 2)
                for c in range(4):
                    at = (c // 2) * SLOTS + i * CAP
                    head = (8 * g + 2 * r + c % 2) * HEAD
                    out_ref[(*to, slice(c * CAP, (c + 1) * CAP), slice(None))] = queries[
                        at : at + CAP, head : head + HEAD
                    ]
                at = (r % 2) * SLOTS + i * CAP
                lanes = slice(g * HEAD, (g + 1) * HEAD)
                out_ref[(*to, slice(4 * CAP, 5 * CAP), slice(None))] = keys[at : at + CAP, lanes]
                out_ref[(*to, slice(5 * CAP, 6 * CAP), slice(None))] = values[at : at + CAP, lanes]
                out_ref[(*to, slice(SENT, CHUNK), slice(None))] = label_ref[i]


def pack(turn, facts, target, block, q, k, v):
    rows, place = pl.pallas_call(
        functools.partial(pack_kernel, turn),
        grid=(KEY_HEADS // GROUP,),
        in_specs=[
            pl.BlockSpec(memory_space=pltpu.SMEM),
            pl.BlockSpec((1, ROWS // 2), lambda g: (0, 0)),
            pl.BlockSpec((1, ROWS // 2), lambda g: (0, 0)),
            pl.BlockSpec((ROWS, WIDE), lambda g: (0, g)),
            pl.BlockSpec((ROWS, GROUP * HEAD), lambda g: (0, g)),
            pl.BlockSpec((ROWS, GROUP * HEAD), lambda g: (0, g)),
        ],
        out_specs=(
            pl.BlockSpec((2, 2, 2, GROUP, 2, CHUNK, HEAD), lambda g: (0, 0, 0, g, 0, 0, 0)),
            pl.BlockSpec((ROWS, ROWS), lambda g: (0, 0)),
        ),
        out_shape=(
            jax.ShapeDtypeStruct((2, 2, 2, KEY_HEADS, 2, CHUNK, HEAD), BF16),
            jax.ShapeDtypeStruct((ROWS, ROWS), BF16),
        ),
        scratch_shapes=[pltpu.VMEM((ROWS, ROWS), BF16), pltpu.VMEM((INSTANCES, 8, ROWS), BF16)],
        compiler_params=ROOM,
        name="pack",
    )(facts, target, block, q, k, v)
    return rows.reshape(DEVICES, CHUNK, HEAD), place


def slot_positions(turn, rows_ref):
    label = rows_ref[:, SENT:CHUNK, :].astype(F32).reshape(DEVICES // 8, 8, 8, HEAD)
    label = jnp.sum(label, axis=1)
    row = lax.broadcasted_iota(jnp.int32, label.shape, 1)
    part = jnp.where(row == 2 * turn, label * 64.0, jnp.where(row == 2 * turn + 1, label, 0.0))
    return jnp.sum(part, axis=1) - 1.0


def line_up(pos):
    return jnp.concatenate([pos[j : j + 1] for j in range(DEVICES // 8)], axis=1)


def sorted_pair(line_ref, rows_refs, c):
    slots = DEVICES * CAP
    wanted = lax.broadcasted_iota(jnp.int32, (SORTED, slots), 0) + pl.program_id(0) * SORTED
    found = None
    for turn, rows_ref in enumerate(rows_refs):
        pick = jnp.where(line_ref[turn, 0:1, :] == wanted, 1.0, 0.0).astype(BF16)
        pair = [rows_ref[:, p * CAP : (p + 1) * CAP, :].reshape(slots, HEAD) for p in (c, c + 1)]
        added = jnp.dot(pick, jnp.concatenate(pair, axis=1), preferred_element_type=F32)
        found = added if found is None else found + added
    return found


def sort_keys_kernel(rounds, *refs):
    rows_refs = refs[:rounds]
    keys_ref, values_ref, line_ref, column_ref, most_ref = refs[rounds:]

    @pl.when(pl.program_id(0) == 0)
    def _():
        for turn in range(rounds):
            pos = slot_positions(turn, rows_refs[0])
            line_ref[turn] = jnp.broadcast_to(line_up(pos).astype(jnp.int32), (8, DEVICES * CAP))
            empty = jnp.zeros((HEAD - DEVICES // 8, HEAD), F32)
            column_ref[turn] = jnp.concatenate([pos, empty], axis=0).T
        count = rows_refs[0][:, SENT:CHUNK, :].astype(F32)
        row = lax.broadcasted_iota(jnp.int32, count.shape, 1)
        most_ref[0] = jnp.max(jnp.where(row == 4, count, 0.0)).astype(jnp.int32)

    found = sorted_pair(line_ref, rows_refs, 4)
    keys_ref[...] = found[:, :HEAD].astype(BF16)
    values_ref[...] = found[:, HEAD:].T.astype(BF16)


def sort_keys(rows):
    rounds, slots = len(rows), DEVICES * CAP
    line, column = (rounds, 8, slots), (rounds, HEAD, HEAD)
    return pl.pallas_call(
        functools.partial(sort_keys_kernel, rounds),
        grid=(SEQ_BLOCKS // SORTED,),
        in_specs=[pl.BlockSpec((DEVICES, CHUNK, HEAD), lambda t: (0, 0, 0))] * rounds,
        out_specs=(
            pl.BlockSpec((SORTED, HEAD), lambda t: (t, 0)),
            pl.BlockSpec((HEAD, SORTED), lambda t: (0, t)),
            pl.BlockSpec(line, lambda t: (0, 0, 0)),
            pl.BlockSpec(column, lambda t: (0, 0, 0)),
            pl.BlockSpec(memory_space=pltpu.SMEM),
        ),
        out_shape=(
            jax.ShapeDtypeStruct((SEQ_BLOCKS, HEAD), BF16),
            jax.ShapeDtypeStruct((HEAD, SEQ_BLOCKS), BF16),
            jax.ShapeDtypeStruct(line, jnp.int32),
            jax.ShapeDtypeStruct(column, F32),
            jax.ShapeDtypeStruct((1,), jnp.int32),
        ),
        compiler_params=ROOM,
        name="sort_keys",
    )(*rows)


def sort_queries_kernel(line_ref, *refs):
    out_ref = refs[-1]
    for c in range(0, 4, 2):
        found = sorted_pair(line_ref, refs[:-1], c).astype(BF16)
        out_ref[c] = found[:, :HEAD]
        out_ref[c + 1] = found[:, HEAD:]


def sort_queries(line, rows):
    flops = 2 * SEQ_BLOCKS * DEVICES * CAP * len(rows) * 4 * HEAD
    return pl.pallas_call(
        sort_queries_kernel,
        grid=(SEQ_BLOCKS // SORTED,),
        in_specs=[pl.BlockSpec(line.shape, lambda t: (0, 0, 0))]
        + [pl.BlockSpec((DEVICES, 4 * CAP, HEAD), lambda t: (0, 0, 0))] * len(rows),
        out_specs=pl.BlockSpec((4, SORTED, HEAD), lambda t: (0, t, 0)),
        out_shape=jax.ShapeDtypeStruct((4, SEQ_BLOCKS, HEAD), BF16),
        compiler_params=ROOM,
        cost_estimate=pl.CostEstimate(flops=flops, bytes_accessed=4 << 20, transcendentals=0),
        name="sort_queries",
    )(line, *rows)


def attend_tile(
    shift, tile, facts_ref, q_ref, own_keys, own_values, other_keys, other_values, out_ref, sum_ref, extra_ref
):
    core = facts_ref[0]
    span = 2 * TILE
    columns = 4 * TILE
    first = tile * span
    queries_ref = q_ref.at[:, pl.ds(pl.multiple_of(tile % TURNS * TILE, TILE), TILE), :]

    def start_of(position):
        start, end = jnp.zeros_like(position), jnp.int32(0)
        for d in range(2, facts_ref.shape[0]):
            end = end + facts_ref[d]
            start = jnp.where(end <= position, end, start)
        return start

    column = lax.broadcasted_iota(jnp.int32, (1, columns), 1)
    query_pos = first + (column % TILE) * 2 + column // (2 * TILE)
    query_start = start_of(query_pos)

    def key_pos(at, wide, index):
        own = index < wide * TILE
        block = jnp.where(own, index, index - wide * TILE) + at * TILE
        return block * 2 + jnp.where(own, core, 1 - core)

    def scores_of(at, wide):
        at_keys = pl.ds(pl.multiple_of(at * TILE, TILE), wide * TILE)
        keys = jnp.concatenate([own_keys[at_keys, :], other_keys[at_keys, :]], axis=0)
        scores = lax.dot_general(
            keys,
            queries_ref[...].reshape(columns, HEAD),
            (((1,), (1,)), ((), ())),
            preferred_element_type=F32,
        )
        return scores * SCALE

    def allowed_scores(at, whole):
        pos = key_pos(at, 1, lax.broadcasted_iota(jnp.int32, (span, 1), 0))
        allowed = (pos <= query_pos) & (pos >= query_start) if whole else pos <= query_pos
        return jnp.where(allowed, scores_of(at, 1), -1e30)

    def mixed(at, wide, weights, start=None):
        at_keys = pl.ds(pl.multiple_of(at * TILE, TILE), wide * TILE)
        values = jnp.concatenate([own_values[:, at_keys], other_values[:, at_keys]], axis=1)
        ones = jnp.ones((16, wide * span), BF16)
        if start is not None:
            pos = key_pos(at, wide, lax.broadcasted_iota(jnp.int32, (16, wide * span), 1))
            ones = jnp.where(pos >= start, 1.0, 0.0).astype(BF16)
            values = values * ones[0:1]
        values = jnp.concatenate([values, ones], axis=0)
        return jnp.dot(values, weights.astype(BF16), preferred_element_type=F32)

    start = start_of(first)
    low = start // span

    if shift:

        def shifted(at, begins):
            scores = allowed_scores(at, True)
            best = jnp.broadcast_to(jnp.max(scores, axis=0, keepdims=True), (8, columns))
            top = best if begins else jnp.maximum(extra_ref[...], best)
            added = mixed(at, 1, jnp.exp2(scores - top[0:1]))
            if begins:
                sum_ref[...] = added
            else:
                sum_ref[...] = sum_ref[...] * jnp.exp2(extra_ref[0:1] - top[0:1]) + added
            extra_ref[...] = top

        shifted(tile, True)

        @pl.loop(low, tile)
        def _(at):
            shifted(at, False)

    else:
        sum_ref[...] = jnp.zeros_like(sum_ref)
        left = tile - low
        for wide in (1, 2, 4):

            @pl.when((left // wide) % 2 == 1)
            def _():
                at = low + left % wide
                sum_ref[...] += mixed(at, wide, jnp.exp2(scores_of(at, wide)), start)

        split = start_of(first + span - 1) > first

        @pl.when(split)
        def _():
            added = mixed(tile, 1, jnp.exp2(allowed_scores(tile, True)))
            sum_ref[...] = jnp.where(query_start <= first, sum_ref[...], 0.0) + added

        @pl.when(jnp.logical_not(split))
        def _():
            sum_ref[...] += mixed(tile, 1, jnp.exp2(allowed_scores(tile, False)))

        total = sum_ref[HEAD : HEAD + 8]
        extra_ref[...] += jnp.where((total <= 2.0**100) & (total >= 2.0**-80), 0.0, 1.0)

    done = (sum_ref[:HEAD] / sum_ref[HEAD : HEAD + 1]).astype(BF16)
    place = pl.ds(pl.multiple_of(tile * TILE, TILE), TILE)
    for c in range(4):
        out_ref[c * HEAD : (c + 1) * HEAD, place] = done[:, c * TILE : (c + 1) * TILE]


def unsort_tile(step, column_ref, attended_ref, out_ref):
    lane = lax.broadcasted_iota(jnp.int32, (HEAD, HEAD), 1)
    turn, near = step // UNSORTS, step % UNSORTS
    wide = UNSORTED // HEAD
    columns = [
        jnp.sum(jnp.where(lane == near * wide + j, column_ref[turn], 0.0), axis=1, keepdims=True)
        for j in range(wide)
    ]
    pos = jnp.concatenate(columns, axis=0).astype(jnp.int32)
    block = lax.broadcasted_iota(jnp.int32, (UNSORTED, SEQ_BLOCKS), 1)
    pick = jnp.where(pos == block, 1.0, 0.0).astype(BF16)
    for c in range(0, 4, 2):
        found = lax.dot_general(
            pick,
            attended_ref[c * HEAD : (c + 2) * HEAD, :],
            (((1,), (1,)), ((), ())),
            preferred_element_type=F32,
        ).astype(BF16)
        for p in range(2):
            part = found[:, p * HEAD : (p + 1) * HEAD].reshape(UNSORTED // CAP, CAP, HEAD)
            out_ref[:, (c + p) * CAP : (c + p + 1) * CAP, :] = part


def attend_kernel(facts_ref, column_ref, q_ref, *refs):
    key_refs, out_ref, attended_ref, more = refs[:4], refs[4], refs[5], refs[6:]
    step = pl.program_id(0)

    def attend_tiles(shift):
        @pl.loop(step * TURNS, (step + 1) * TURNS)
        def _(tile):
            attend_tile(shift, tile, facts_ref, q_ref, *key_refs, attended_ref, *more)

    @pl.when(step < TILES // TURNS)
    def _():
        extra_ref = more[1]
        extra_ref[...] = jnp.zeros_like(extra_ref)
        attend_tiles(False)

        @pl.when(jnp.max(extra_ref[...]) > 0.0)
        def _():
            attend_tiles(True)

    @pl.when(step >= TILES // TURNS)
    def _():
        unsort_tile(step - TILES // TURNS, column_ref, attended_ref, out_ref)


def attend(facts, column, queries, own, other):
    rounds, steps = column.shape[0], TILES // TURNS
    keys = pl.BlockSpec((SEQ_BLOCKS, HEAD), lambda t: (0, 0))
    values = pl.BlockSpec((HEAD, SEQ_BLOCKS), lambda t: (0, 0))
    return pl.pallas_call(
        attend_kernel,
        grid=(steps + rounds * UNSORTS,),
        in_specs=[
            pl.BlockSpec(memory_space=pltpu.SMEM),
            pl.BlockSpec(column.shape, lambda t: (0, 0, 0)),
            pl.BlockSpec((4, TURNS * TILE, HEAD), lambda t: (0, jnp.minimum(t, steps - 1), 0)),
            keys,
            values,
            keys,
            values,
        ],
        out_specs=pl.BlockSpec(
            (UNSORTED // CAP, BACK, HEAD), lambda t: (jnp.maximum(t - steps, 0), 0, 0)
        ),
        out_shape=jax.ShapeDtypeStruct((rounds * DEVICES, BACK, HEAD), BF16),
        scratch_shapes=[
            pltpu.VMEM((4 * HEAD, SEQ_BLOCKS), BF16),
            pltpu.VMEM((HEAD + 16, 4 * TILE), F32),
            pltpu.VMEM((8, 4 * TILE), F32),
        ],
        compiler_params=ROOM,
        name="attend",
    )(facts, column, queries, *own, *other)


def unpack_kernel(rounds, *refs):
    place_refs, back_refs, out_ref = refs[:rounds], refs[rounds:-1], refs[-1]
    total = jnp.zeros(out_ref.shape, F32)
    for turn in range(rounds):
        lines = []
        for parity in range(2):
            for i in range(INSTANCES):
                line = []
                for g in range(GROUP):
                    for r in range(4):
                        of = (i // 2, r % 2, i % 2, g, r // 2)
                        for h in range(2):
                            at = (2 * parity + h) * CAP
                            line.append(back_refs[turn][(*of, slice(at, at + CAP), slice(None))])
                lines.append(jnp.concatenate(line, axis=1))
        total = total + jnp.dot(
            place_refs[turn][...], jnp.concatenate(lines, axis=0), preferred_element_type=F32
        )
    out_ref[...] = total.astype(BF16)


def unpack(places, backs):
    rounds = len(backs)
    block = pl.BlockSpec((2, 2, 2, GROUP, 2, BACK, HEAD), lambda g: (0, 0, 0, g, 0, 0, 0))
    return pl.pallas_call(
        functools.partial(unpack_kernel, rounds),
        grid=(KEY_HEADS // GROUP,),
        in_specs=[pl.BlockSpec((ROWS, ROWS), lambda g: (0, 0))] * rounds + [block] * rounds,
        out_specs=pl.BlockSpec((ROWS, WIDE), lambda g: (0, g)),
        out_shape=jax.ShapeDtypeStruct((ROWS, KEY_HEADS * 8 * HEAD), BF16),
        compiler_params=ROOM,
        name="unpack",
    )(*places, *(b.reshape(2, 2, 2, KEY_HEADS, 2, BACK, HEAD) for b in backs))


def exchange(x):
    return lax.all_to_all(x, BOTH, split_axis=0, concat_axis=0, tiled=True)


def shards(query_rows, key_rows, value_rows, target_instance, block_position, request_lengths):
    spot, place = lax.axis_index("inst"), lax.axis_index("seq")
    core = spot % 2
    instance = (spot // 2) * 2 + place // 16
    lengths = lax.dynamic_index_in_dim(request_lengths, instance, 0, keepdims=False)
    facts = jnp.concatenate([jnp.stack([core, (place % 8) * CAP]), lengths]).astype(jnp.int32)
    plan = (facts, target_instance[None, :], block_position[None, :])

    def run(rounds):
        packed = [pack(t, *plan, query_rows, key_rows, value_rows) for t in range(rounds)]
        rows = [exchange(sent) for sent, _ in packed]
        keys, values, line, column, most = sort_keys(rows)
        pairs = [(0, 1), (1, 0), (2, 3), (3, 2)]
        other = [lax.ppermute(x, "inst", pairs) for x in (keys, values)]
        back = attend(facts, column, sort_queries(line, rows), (keys, values), other)
        backs = [exchange(back[t * DEVICES : (t + 1) * DEVICES]) for t in range(rounds)]
        return unpack([places for _, places in packed], backs), most[0]

    attended, most = run(1)
    return lax.while_loop(
        lambda state: state[1] > CAP,
        lambda state: (run(2)[0], jnp.zeros_like(state[1])),
        (attended, most),
    )[0]


def solution(mesh):
    rows = P(BOTH, None)
    return jax.shard_map(
        shards,
        mesh=mesh,
        in_specs=(rows, rows, rows, P(BOTH), P(BOTH), P()),
        out_specs=rows,
        check_vma=False,
    )
```

time: 184 us -> 162 us (0.88); the launches traced: 184 us -> 165 us
  Pallas kernels: 87.3 us -> 72.1 us
  blocking collectives: 91.9 us -> 89.7 us
    pallas_call x1, Pallas kernels: 64 us -> 58.7 us  [attend(): pl.pallas_call(attend_kernel, grid=(steps + rounds * UNSORTS,), in_specs=...]
    pallas_call x1, Pallas kernels: 6.16 us -> 3.51 us  [sort_keys(): pl.pallas_call(functools.partial(sort_keys_kernel, rounds), grid=(SEQ_BLO...]
    pallas_call x1, Pallas kernels: 4.62 us -> 1.99 us  [unpack(): pl.pallas_call(functools.partial(unpack_kernel, rounds), grid=(KEY_HEADS...]
    pallas_call x1, Pallas kernels: 7.51 us -> 4.91 us  [sort_queries(): pl.pallas_call(sort_queries_kernel, grid=(SEQ_BLOCKS // SORTED,), in_spec...]
    all_to_all x2, blocking collectives: 91.9 us -> 89.7 us  [exchange(): return lax.all_to_all(x, BOTH, split_axis=0, concat_axis=0, tiled=True)]
    pallas_call x1, Pallas kernels: 4.99 us -> 2.99 us  [pack(): pl.pallas_call(functools.partial(pack_kernel, turn), grid=(KEY_HEADS // G...]
  transfers between devices with their start and end apart: 2 -> 2, of which waited for: 0 -> 0; matrix products, arithmetic and copies ran while one was open for 0% -> 0% of each run, Pallas kernels for 4% -> 3%
where the time goes in v3:
time: 162 us; the launch traced here: 165 us
  blocking collectives  89.7 us (55%)
  Pallas kernels  72.1 us (45%)
    all_to_all x2, blocking collectives, exchange(): return lax.all_to_all(x, BOTH, split_axis=0, concat_axis=0, tiled=True)  89.7 us
    pallas_call x1, Pallas kernels, attend(): pl.pallas_call(attend_kernel, grid=(steps + rounds * UNSORTS,), in_specs=...  58.7 us
    pallas_call x1, Pallas kernels, sort_queries(): pl.pallas_call(sort_queries_kernel, grid=(SEQ_BLOCKS // SORTED,), in_spec...  4.91 us
    pallas_call x1, Pallas kernels, sort_keys(): pl.pallas_call(functools.partial(sort_keys_kernel, rounds), grid=(SEQ_BLO...  3.51 us
  transfers between devices with their start and end apart: 2, of which 0 were waited for; matrix products, arithmetic and copies ran while one was open for 0% of the time, Pallas kernels for 3%

profile of v3, /device:TPU:1, one launch (start us, length us, event | category | flops | bytes accessed | tf_op | source)
XLA Modules:
  0.0 165.2 jit_solution(13982294609007050157)
XLA Ops:
  0.0 0.0 copy-start
  0.0 0.7 copy-done
  0.7 0.2 dynamic-slice_reduce_fusion
  0.9 0.1 pad_add_fusion.facts_ref
  0.9 3.0 %pack.5 = (bf16[2,2,2,8,2,104,128]{6,5,4,3,2,1,0:T(8,128)(2,1)S(1)}, bf16[128,128]{1,0:T(8,128)(2,1)S(1)}) custom-call(s32[4]{0:T(128)S(1)} %pad_add_fusion.facts_ref, s32[1,64]{1,0:T(1,128)} %bitcast.16, s32[1,64]{1,0:T(1,128)} %bitcast.18, bf16[128,8192]{1,0:T(8,128)(2,1)} %q_ref.1, bf16[128,1024]{1,0:T(8,128)(2,1)} %k_ref.1, bf16[128,1024]{1,0:T(8,128)(2,1)} %v_ref.1), custom_call_target="tpu_custom_call" | custom-call | tf_op jit(solution)/shard_map/pack/pallas_call | solution.py:95
  3.9 56.0 %all_to_all.28.refs_0_ = bf16[128,104,128]{2,1,0:T(8,128)(2,1)S(1)} all-to-all(bf16[128,104,128]{2,1,0:T(8,128)(2,1)S(1)} %bitcast.15), channel_id=1, replica_groups=mesh['inst'=4,'seq'=32] {'inst','seq'}, dimensions={0} | all-to-all | bytes 6815744 | tf_op jit(solution)/shard_map/all_to_all | solution.py:431
  59.9 3.5 %sort_keys.3 = (bf16[2048,128]{1,0:T(8,128)(2,1)S(1)}, bf16[128,2048]{1,0:T(8,128)(2,1)S(1)}, s32[1,8,2048]{2,1,0:T(8,128)S(1)}, f32[1,128,128]{2,1,0:T(8,128)S(1)}, s32[1]{0:T(128)}) custom-call(bf16[128,104,128]{2,1,0:T(8,128)(2,1)S(1)} %all_to_all.28.refs_0_), custom_call_target="tpu_custom_call" | custom-call | tf_op jit(solution)/shard_map/sort_keys/pallas_call | solution.py:168
  63.4 1.2 collective-permute-start.2
  64.7 0.3 collective-permute-start.3
  64.9 4.9 %sort_queries.3.q_ref = bf16[4,2048,128]{2,1,0:T(8,128)(2,1)S(1)} custom-call(s32[1,8,2048]{2,1,0:T(8,128)S(1)} %get-tuple-element.63.line_ref, bf16[128,104,128]{2,1,0:T(8,128)(2,1)S(1)} %all_to_all.28.refs_0_), custom_call_target="tpu_custom_call" | custom-call | flops 4294967296 | bytes 4194304 | tf_op jit(solution)/shard_map/sort_queries/pallas_call | solution.py:201
  69.8 0.0 collective-permute-done.2.refs_2_
  69.9 0.0 collective-permute-done.3.refs_3_
  69.9 58.7 %attend.3 = bf16[128,64,128]{2,1,0:T(8,128)(2,1)S(1)} custom-call(s32[4]{0:T(128)S(1)} %pad_add_fusion.facts_ref, f32[1,128,128]{2,1,0:T(8,128)S(1)} %get-tuple-element.62.column_ref, bf16[4,2048,128]{2,1,0:T(8,128)(2,1)S(1)} %sort_queries.3.q_ref, bf16[2048,128]{1,0:T(8,128)(2,1)S(1)} %get-tuple-element.64.refs_0_, ...), custom_call_target="tpu_custom_call" | custom-call | tf_op jit(solution)/shard_map/attend/pallas_call | solution.py:369
  128.6 33.8 %all_to_all.29 = bf16[128,64,128]{2,1,0:T(8,128)(2,1)S(1)} all-to-all(bf16[128,64,128]{2,1,0:T(8,128)(2,1)S(1)} %attend.3), channel_id=1, replica_groups=mesh['inst'=4,'seq'=32] {'inst','seq'}, dimensions={0} | all-to-all | bytes 4194304 | tf_op jit(solution)/shard_map/all_to_all | solution.py:431
  162.4 0.0 copy-start.3
  162.4 0.0 copy-start.4
  162.4 2.0 %unpack.3 = bf16[128,8192]{1,0:T(8,128)(2,1)} custom-call(bf16[128,128]{1,0:T(8,128)(2,1)S(1)} %get-tuple-element.60.refs_0_, bf16[2,2,2,8,2,64,128]{6,5,4,3,2,1,0:T(8,128)(2,1)S(1)} %bitcast.14), custom_call_target="tpu_custom_call" | custom-call | tf_op jit(solution)/shard_map/unpack/pallas_call | solution.py:419
  164.3 0.0 copy-done.3
  164.4 0.0 copy-done.4
  164.4 0.7 while.9
Async XLA Ops:
  0.0 0.7 copy-start
  63.4 6.4 %collective-permute-start.2 = (bf16[2048,128]{1,0:T(8,128)(2,1)S(1)}, bf16[2048,128]{1,0:T(8,128)(2,1)S(1)}, u32[]{:S(2)}, u32[]{:S(2)}) collective-permute-start(bf16[2048,128]{1,0:T(8,128)(2,1)S(1)} %get-tuple-element.64.refs_0_), channel_id=1, source_target_pairs={{0,32},{32,0},{64,96},{96,64},{1,33},{33,1},{65,97},{97,65},{2,34}... | collective-permute-start | bytes 1572872 | tf_op jit(solution)/shard_map/ppermute | solution.py:447
  64.7 5.2 %collective-permute-start.3 = (bf16[128,2048]{1,0:T(8,128)(2,1)S(1)}, bf16[128,2048]{1,0:T(8,128)(2,1)S(1)}, u32[]{:S(2)}, u32[]{:S(2)}) collective-permute-start(bf16[128,2048]{1,0:T(8,128)(2,1)S(1)} %get-tuple-element.65.refs_1_), channel_id=1, source_target_pairs={{0,32},{32,0},{64,96},{96,64},{1,33},{33,1},{65,97},{97,65},{2,34}... | collective-permute-start | bytes 1572872 | tf_op jit(solution)/shard_map/ppermute | solution.py:447
  162.4 2.0 %copy-start.3 = (s32[64]{0:T(128)S(1)}, s32[64]{0:T(128)}, u32[]{:S(2)}) copy-start(s32[64]{0:T(128)} %param.11) | copy-start | bytes 772
  162.4 2.0 %copy-start.4 = (s32[64]{0:T(128)S(1)}, s32[64]{0:T(128)}, u32[]{:S(2)}) copy-start(s32[64]{0:T(128)} %param.12) | copy-start | bytes 772

commit v4 on v3

--- a/solution.py
+++ b/solution.py
@@ -20,8 +20,7 @@
 TILE = 256
 TILES = SEQ_BLOCKS // TILE
 SORTED = 1024
-TURNS = 2
-UNSORTED = 1024
+UNSORTED = 512
 UNSORTS = DEVICES * CAP // UNSORTED
 SENT = 6 * CAP
 CHUNK = SENT + 8
@@ -29,12 +28,14 @@
 GROUP = 4
 WIDE = GROUP * 8 * HEAD
 SCALE = math.log2(math.e) / math.sqrt(HEAD)
-ROOM = pltpu.CompilerParams(vmem_limit_bytes=36 << 20)
+HERE = pl.BlockSpec(memory_space=pltpu.VMEM)
+NEAR = pl.BlockSpec(memory_space=pltpu.SMEM)
+ROOM = pltpu.CompilerParams(vmem_limit_bytes=28 << 20)
 F32 = jnp.float32
 BF16 = jnp.bfloat16
 
 
-def plan_pack(turn, facts_ref, target_ref, block_ref, pick_ref, label_ref, place_ref):
+def plan_pack(turn, offset_ref, target_ref, block_ref, pick_ref, label_ref, place_ref):
     shape = (ROWS, ROWS)
     half = jnp.full((1, ROWS // 2), -1.0, F32)
     inst_l = jnp.concatenate([target_ref[...].astype(F32), half], axis=1)
@@ -53,7 +54,7 @@
     place_ref[...] = pick.T.astype(BF16)
     most = jnp.max(jnp.broadcast_to(rank, shape), axis=0, keepdims=True) + 1.0
     row = sub[:8]
-    at = lane - facts_ref[1]
+    at = lane - offset_ref[0]
     for i in range(INSTANCES):
         label = jnp.where(row == 4, most, 0.0)
         for t in range(2):
@@ -65,10 +66,10 @@
         label_ref[i] = label.astype(BF16)
 
 
-def pack_kernel(turn, facts_ref, target_ref, block_ref, q_ref, k_ref, v_ref, out_ref, place_ref, pick_ref, label_ref):
+def pack_kernel(turn, offset_ref, target_ref, block_ref, q_ref, k_ref, v_ref, out_ref, place_ref, pick_ref, label_ref):
     @pl.when(pl.program_id(0) == 0)
     def _():
-        plan_pack(turn, facts_ref, target_ref, block_ref, pick_ref, label_ref, place_ref)
+        plan_pack(turn, offset_ref, target_ref, block_ref, pick_ref, label_ref, place_ref)
 
     pick = pick_ref[...]
     queries = jnp.dot(pick, q_ref[...], preferred_element_type=F32).astype(BF16)
@@ -91,12 +92,12 @@
                 out_ref[(*to, slice(SENT, CHUNK), slice(None))] = label_ref[i]
 
 
-def pack(turn, facts, target, block, q, k, v):
+def pack(turn, offset, target, block, q, k, v):
     rows, place = pl.pallas_call(
         functools.partial(pack_kernel, turn),
         grid=(KEY_HEADS // GROUP,),
         in_specs=[
-            pl.BlockSpec(memory_space=pltpu.SMEM),
+            NEAR,
             pl.BlockSpec((1, ROWS // 2), lambda g: (0, 0)),
             pl.BlockSpec((1, ROWS // 2), lambda g: (0, 0)),
             pl.BlockSpec((ROWS, WIDE), lambda g: (0, g)),
@@ -114,7 +115,7 @@
         scratch_shapes=[pltpu.VMEM((ROWS, ROWS), BF16), pltpu.VMEM((INSTANCES, 8, ROWS), BF16)],
         compiler_params=ROOM,
         name="pack",
-    )(facts, target, block, q, k, v)
+    )(offset, target, block, q, k, v)
     return rows.reshape(DEVICES, CHUNK, HEAD), place
 
 
@@ -127,15 +128,15 @@
 
 
 def line_up(pos):
-    return jnp.concatenate([pos[j : j + 1] for j in range(DEVICES // 8)], axis=1)
-
-
-def sorted_pair(line_ref, rows_refs, c):
+    return jnp.concatenate([pos[j : j + 1] for j in range(DEVICES // 8)], axis=1).astype(jnp.int32)
+
+
+def sorted_pair(first, lines, rows_refs, c):
     slots = DEVICES * CAP
-    wanted = lax.broadcasted_iota(jnp.int32, (SORTED, slots), 0) + pl.program_id(0) * SORTED
+    wanted = lax.broadcasted_iota(jnp.int32, (SORTED, slots), 0) + first
     found = None
     for turn, rows_ref in enumerate(rows_refs):
-        pick = jnp.where(line_ref[turn, 0:1, :] == wanted, 1.0, 0.0).astype(BF16)
+        pick = jnp.where(lines[turn] == wanted, 1.0, 0.0).astype(BF16)
         pair = [rows_ref[:, p * CAP : (p + 1) * CAP, :].reshape(slots, HEAD) for p in (c, c + 1)]
         added = jnp.dot(pick, jnp.concatenate(pair, axis=1), preferred_element_type=F32)
         found = added if found is None else found + added
@@ -144,43 +145,32 @@
 
 def sort_keys_kernel(rounds, *refs):
     rows_refs = refs[:rounds]
-    keys_ref, values_ref, line_ref, column_ref, most_ref = refs[rounds:]
-
-    @pl.when(pl.program_id(0) == 0)
-    def _():
-        for turn in range(rounds):
-            pos = slot_positions(turn, rows_refs[0])
-            line_ref[turn] = jnp.broadcast_to(line_up(pos).astype(jnp.int32), (8, DEVICES * CAP))
-            empty = jnp.zeros((HEAD - DEVICES // 8, HEAD), F32)
-            column_ref[turn] = jnp.concatenate([pos, empty], axis=0).T
-        count = rows_refs[0][:, SENT:CHUNK, :].astype(F32)
-        row = lax.broadcasted_iota(jnp.int32, count.shape, 1)
-        most_ref[0] = jnp.max(jnp.where(row == 4, count, 0.0)).astype(jnp.int32)
-
-    found = sorted_pair(line_ref, rows_refs, 4)
-    keys_ref[...] = found[:, :HEAD].astype(BF16)
-    values_ref[...] = found[:, HEAD:].T.astype(BF16)
+    keys_ref, values_ref, column_ref, most_ref = refs[rounds:]
+    lines = []
+    for turn in range(rounds):
+        pos = slot_positions(turn, rows_refs[0])
+        lines.append(line_up(pos))
+        empty = jnp.zeros((HEAD - DEVICES // 8, HEAD), F32)
+        column_ref[turn] = jnp.concatenate([pos, empty], axis=0).T
+    count = rows_refs[0][:, SENT:CHUNK, :].astype(F32)
+    row = lax.broadcasted_iota(jnp.int32, count.shape, 1)
+    most_ref[0] = jnp.max(jnp.where(row == 4, count, 0.0)).astype(jnp.int32)
+    for first in range(0, SEQ_BLOCKS, SORTED):
+        found = sorted_pair(first, lines, rows_refs, 4)
+        keys_ref[first : first + SORTED] = found[:, :HEAD].astype(BF16)
+        values_ref[:, first : first + SORTED] = found[:, HEAD:].T.astype(BF16)
 
 
 def sort_keys(rows):
-    rounds, slots = len(rows), DEVICES * CAP
-    line, column = (rounds, 8, slots), (rounds, HEAD, HEAD)
+    rounds = len(rows)
     return pl.pallas_call(
         functools.partial(sort_keys_kernel, rounds),
-        grid=(SEQ_BLOCKS // SORTED,),
-        in_specs=[pl.BlockSpec((DEVICES, CHUNK, HEAD), lambda t: (0, 0, 0))] * rounds,
-        out_specs=(
-            pl.BlockSpec((SORTED, HEAD), lambda t: (t, 0)),
-            pl.BlockSpec((HEAD, SORTED), lambda t: (0, t)),
-            pl.BlockSpec(line, lambda t: (0, 0, 0)),
-            pl.BlockSpec(column, lambda t: (0, 0, 0)),
-            pl.BlockSpec(memory_space=pltpu.SMEM),
-        ),
+        in_specs=[HERE] * rounds,
+        out_specs=(HERE, HERE, HERE, NEAR),
         out_shape=(
             jax.ShapeDtypeStruct((SEQ_BLOCKS, HEAD), BF16),
             jax.ShapeDtypeStruct((HEAD, SEQ_BLOCKS), BF16),
-            jax.ShapeDtypeStruct(line, jnp.int32),
-            jax.ShapeDtypeStruct(column, F32),
+            jax.ShapeDtypeStruct((rounds, HEAD, HEAD), F32),
             jax.ShapeDtypeStruct((1,), jnp.int32),
         ),
         compiler_params=ROOM,
@@ -188,27 +178,27 @@
     )(*rows)
 
 
-def sort_queries_kernel(line_ref, *refs):
-    out_ref = refs[-1]
-    for c in range(0, 4, 2):
-        found = sorted_pair(line_ref, refs[:-1], c).astype(BF16)
-        out_ref[c] = found[:, :HEAD]
-        out_ref[c + 1] = found[:, HEAD:]
-
-
-def sort_queries(line, rows):
+def sort_queries_kernel(*refs):
+    rows_refs, out_ref = refs[:-1], refs[-1]
+    lines = [line_up(slot_positions(turn, rows_refs[0])) for turn in range(len(rows_refs))]
+    for first in range(0, SEQ_BLOCKS, SORTED):
+        for c in range(0, 4, 2):
+            found = sorted_pair(first, lines, rows_refs, c).astype(BF16)
+            out_ref[c, first : first + SORTED] = found[:, :HEAD]
+            out_ref[c + 1, first : first + SORTED] = found[:, HEAD:]
+
+
+def sort_queries(rows):
     flops = 2 * SEQ_BLOCKS * DEVICES * CAP * len(rows) * 4 * HEAD
     return pl.pallas_call(
         sort_queries_kernel,
-        grid=(SEQ_BLOCKS // SORTED,),
-        in_specs=[pl.BlockSpec(line.shape, lambda t: (0, 0, 0))]
-        + [pl.BlockSpec((DEVICES, 4 * CAP, HEAD), lambda t: (0, 0, 0))] * len(rows),
-        out_specs=pl.BlockSpec((4, SORTED, HEAD), lambda t: (0, t, 0)),
+        in_specs=[HERE] * len(rows),
+        out_specs=HERE,
         out_shape=jax.ShapeDtypeStruct((4, SEQ_BLOCKS, HEAD), BF16),
         compiler_params=ROOM,
         cost_estimate=pl.CostEstimate(flops=flops, bytes_accessed=4 << 20, transcendentals=0),
         name="sort_queries",
-    )(line, *rows)
+    )(*rows)
 
 
 def attend_tile(
@@ -218,11 +208,11 @@
     span = 2 * TILE
     columns = 4 * TILE
     first = tile * span
-    queries_ref = q_ref.at[:, pl.ds(pl.multiple_of(tile % TURNS * TILE, TILE), TILE), :]
+    queries_ref = q_ref.at[:, pl.ds(pl.multiple_of(tile * TILE, TILE), TILE), :]
 
     def start_of(position):
         start, end = jnp.zeros_like(position), jnp.int32(0)
-        for d in range(2, facts_ref.shape[0]):
+        for d in range(1, facts_ref.shape[0]):
             end = end + facts_ref[d]
             start = jnp.where(end <= position, end, start)
         return start
@@ -286,38 +276,36 @@
             shifted(at, False)
 
     else:
-        sum_ref[...] = jnp.zeros_like(sum_ref)
+        split = start_of(first + span - 1) > first
+
+        @pl.when(split)
+        def _():
+            sum_ref[...] = mixed(tile, 1, jnp.exp2(allowed_scores(tile, True)))
+
+        @pl.when(jnp.logical_not(split))
+        def _():
+            sum_ref[...] = mixed(tile, 1, jnp.exp2(allowed_scores(tile, False)))
+
         left = tile - low
         for wide in (1, 2, 4):
 
             @pl.when((left // wide) % 2 == 1)
             def _():
                 at = low + left % wide
-                sum_ref[...] += mixed(at, wide, jnp.exp2(scores_of(at, wide)), start)
-
-        split = start_of(first + span - 1) > first
-
-        @pl.when(split)
-        def _():
-            added = mixed(tile, 1, jnp.exp2(allowed_scores(tile, True)))
-            sum_ref[...] = jnp.where(query_start <= first, sum_ref[...], 0.0) + added
-
-        @pl.when(jnp.logical_not(split))
-        def _():
-            sum_ref[...] += mixed(tile, 1, jnp.exp2(allowed_scores(tile, False)))
+                added = mixed(at, wide, jnp.exp2(scores_of(at, wide)), start)
+                sum_ref[...] += jnp.where(query_start <= first, added, 0.0)
 
         total = sum_ref[HEAD : HEAD + 8]
         extra_ref[...] += jnp.where((total <= 2.0**100) & (total >= 2.0**-80), 0.0, 1.0)
 
-    done = (sum_ref[:HEAD] / sum_ref[HEAD : HEAD + 1]).astype(BF16)
+    done = (sum_ref[:HEAD] * (1.0 / sum_ref[HEAD : HEAD + 8])[0:1]).astype(BF16)
     place = pl.ds(pl.multiple_of(tile * TILE, TILE), TILE)
     for c in range(4):
         out_ref[c * HEAD : (c + 1) * HEAD, place] = done[:, c * TILE : (c + 1) * TILE]
 
 
-def unsort_tile(step, column_ref, attended_ref, out_ref):
+def unsort_tile(turn, near, column_ref, attended_ref, out_ref):
     lane = lax.broadcasted_iota(jnp.int32, (HEAD, HEAD), 1)
-    turn, near = step // UNSORTS, step % UNSORTS
     wide = UNSORTED // HEAD
     columns = [
         jnp.sum(jnp.where(lane == near * wide + j, column_ref[turn], 0.0), axis=1, keepdims=True)
@@ -335,53 +323,37 @@
         ).astype(BF16)
         for p in range(2):
             part = found[:, p * HEAD : (p + 1) * HEAD].reshape(UNSORTED // CAP, CAP, HEAD)
-            out_ref[:, (c + p) * CAP : (c + p + 1) * CAP, :] = part
+            devices = slice((turn * UNSORTS + near) * UNSORTED // CAP, (turn * UNSORTS + near + 1) * UNSORTED // CAP)
+            out_ref[devices, (c + p) * CAP : (c + p + 1) * CAP, :] = part
 
 
 def attend_kernel(facts_ref, column_ref, q_ref, *refs):
     key_refs, out_ref, attended_ref, more = refs[:4], refs[4], refs[5], refs[6:]
-    step = pl.program_id(0)
 
     def attend_tiles(shift):
-        @pl.loop(step * TURNS, (step + 1) * TURNS)
+        @pl.loop(0, TILES)
         def _(tile):
             attend_tile(shift, tile, facts_ref, q_ref, *key_refs, attended_ref, *more)
 
-    @pl.when(step < TILES // TURNS)
+    extra_ref = more[1]
+    extra_ref[...] = jnp.zeros_like(extra_ref)
+    attend_tiles(False)
+
+    @pl.when(jnp.max(extra_ref[...]) > 0.0)
     def _():
-        extra_ref = more[1]
-        extra_ref[...] = jnp.zeros_like(extra_ref)
-        attend_tiles(False)
-
-        @pl.when(jnp.max(extra_ref[...]) > 0.0)
-        def _():
-            attend_tiles(True)
-
-    @pl.when(step >= TILES // TURNS)
-    def _():
-        unsort_tile(step - TILES // TURNS, column_ref, attended_ref, out_ref)
+        attend_tiles(True)
+
+    for turn in range(column_ref.shape[0]):
+        for near in range(UNSORTS):
+            unsort_tile(turn, near, column_ref, attended_ref, out_ref)
 
 
 def attend(facts, column, queries, own, other):
-    rounds, steps = column.shape[0], TILES // TURNS
-    keys = pl.BlockSpec((SEQ_BLOCKS, HEAD), lambda t: (0, 0))
-    values = pl.BlockSpec((HEAD, SEQ_BLOCKS), lambda t: (0, 0))
     return pl.pallas_call(
         attend_kernel,
-        grid=(steps + rounds * UNSORTS,),
-        in_specs=[
-            pl.BlockSpec(memory_space=pltpu.SMEM),
-            pl.BlockSpec(column.shape, lambda t: (0, 0, 0)),
-            pl.BlockSpec((4, TURNS * TILE, HEAD), lambda t: (0, jnp.minimum(t, steps - 1), 0)),
-            keys,
-            values,
-            keys,
-            values,
-        ],
-        out_specs=pl.BlockSpec(
-            (UNSORTED // CAP, BACK, HEAD), lambda t: (jnp.maximum(t - steps, 0), 0, 0)
-        ),
-        out_shape=jax.ShapeDtypeStruct((rounds * DEVICES, BACK, HEAD), BF16),
+        in_specs=[NEAR] + [HERE] * 6,
+        out_specs=HERE,
+        out_shape=jax.ShapeDtypeStruct((column.shape[0] * DEVICES, BACK, HEAD), BF16),
         scratch_shapes=[
             pltpu.VMEM((4 * HEAD, SEQ_BLOCKS), BF16),
             pltpu.VMEM((HEAD + 16, 4 * TILE), F32),
@@ -436,16 +408,16 @@
     core = spot % 2
     instance = (spot // 2) * 2 + place // 16
     lengths = lax.dynamic_index_in_dim(request_lengths, instance, 0, keepdims=False)
-    facts = jnp.concatenate([jnp.stack([core, (place % 8) * CAP]), lengths]).astype(jnp.int32)
-    plan = (facts, target_instance[None, :], block_position[None, :])
+    facts = jnp.concatenate([core[None], lengths]).astype(jnp.int32)
+    plan = ((place % 8 * CAP)[None], target_instance[None, :], block_position[None, :])
 
     def run(rounds):
         packed = [pack(t, *plan, query_rows, key_rows, value_rows) for t in range(rounds)]
         rows = [exchange(sent) for sent, _ in packed]
-        keys, values, line, column, most = sort_keys(rows)
+        keys, values, column, most = sort_keys(rows)
         pairs = [(0, 1), (1, 0), (2, 3), (3, 2)]
         other = [lax.ppermute(x, "inst", pairs) for x in (keys, values)]
-        back = attend(facts, column, sort_queries(line, rows), (keys, values), other)
+        back = attend(facts, column, sort_queries(rows), (keys, values), other)
         backs = [exchange(back[t * DEVICES : (t + 1) * DEVICES]) for t in range(rounds)]
         return unpack([places for _, places in packed], backs), most[0]
 

time: 162 us -> 164 us (1.012); the launches traced: 165 us -> 164 us
  Pallas kernels: 72.1 us -> 61.8 us
  blocking collectives: 89.7 us -> 99.1 us
    pallas_call x3, Pallas kernels: 67.1 us -> 56.9 us  [the longest x1 49.1 us: attend(): pl.pallas_call(attend_kernel, in_specs=[NEAR] + [HERE] * 6, out_specs=HER...]
    all_to_all x2, blocking collectives: 89.7 us -> 99.1 us  [exchange(): return lax.all_to_all(x, BOTH, split_axis=0, concat_axis=0, tiled=True)]
where the time goes in v4:
time: 164 us
  blocking collectives  99.1 us (60%)
  Pallas kernels  61.8 us (38%)
    all_to_all x2, blocking collectives, exchange(): return lax.all_to_all(x, BOTH, split_axis=0, concat_axis=0, tiled=True)  99.1 us
    pallas_call x1, Pallas kernels, attend(): pl.pallas_call(attend_kernel, in_specs=[NEAR] + [HERE] * 6, out_specs=HER...  49.1 us
    pallas_call x1, Pallas kernels, sort_queries(): pl.pallas_call(sort_queries_kernel, in_specs=[HERE] * len(rows), out_spec...  4.49 us
    pallas_call x1, Pallas kernels, sort_keys(): pl.pallas_call(functools.partial(sort_keys_kernel, rounds), in_specs=[HER...  3.31 us
  transfers between devices with their start and end apart: 2, of which 0 were waited for; matrix products, arithmetic and copies ran while one was open for 0% of the time, Pallas kernels for 3%

profile of v4, /device:TPU:1, one launch (start us, length us, event | category | flops | bytes accessed | tf_op | source)
XLA Modules:
  0.0 163.7 jit_solution(12065144017730335126)
XLA Ops:
  0.0 0.0 copy-start
  0.0 3.0 %pack.5 = (bf16[2,2,2,8,2,104,128]{6,5,4,3,2,1,0:T(8,128)(2,1)S(1)}, bf16[128,128]{1,0:T(8,128)(2,1)S(1)}) custom-call(s32[1]{0:T(128)} %bitcast.4.offset_ref, s32[1,64]{1,0:T(1,128)} %bitcast.16, s32[1,64]{1,0:T(1,128)} %bitcast.18, bf16[128,8192]{1,0:T(8,128)(2,1)} %q_ref.1, bf16[128,1024]{1,0:T(8,128)(2,1)} %k_ref.1, bf16[128,1024]{1,0:T(8,128)(2,1)} %v_ref.1), custom_call_target="tpu_custom_call" | custom-call | tf_op jit(solution)/shard_map/pack/pallas_call | solution.py:96
  3.0 56.0 %all_to_all.28.refs_0_ = bf16[128,104,128]{2,1,0:T(8,128)(2,1)S(1)} all-to-all(bf16[128,104,128]{2,1,0:T(8,128)(2,1)S(1)} %bitcast.15), channel_id=1, replica_groups=mesh['inst'=4,'seq'=32] {'inst','seq'}, dimensions={0} | all-to-all | bytes 6815744 | tf_op jit(solution)/shard_map/all_to_all | solution.py:403
  58.9 3.3 %sort_keys.3 = (bf16[2048,128]{1,0:T(8,128)(2,1)}, bf16[128,2048]{1,0:T(8,128)(2,1)}, f32[1,128,128]{2,1,0:T(8,128)S(1)}, s32[1]{0:T(128)}) custom-call(bf16[128,104,128]{2,1,0:T(8,128)(2,1)S(1)} %all_to_all.28.refs_0_), custom_call_target="tpu_custom_call" | custom-call | tf_op jit(solution)/shard_map/sort_keys/pallas_call | solution.py:166
  62.3 1.2 collective-permute-start.2
  63.5 0.1 collective-permute-start.3
  63.6 0.0 copy-done
  63.6 0.2 dynamic-slice_reduce_fusion
  63.8 0.1 pad_add_fusion.facts_ref
  63.9 4.5 %sort_queries.3.q_ref = bf16[4,2048,128]{2,1,0:T(8,128)(2,1)S(1)} custom-call(bf16[128,104,128]{2,1,0:T(8,128)(2,1)S(1)} %all_to_all.28.refs_0_), custom_call_target="tpu_custom_call" | custom-call | flops 4294967296 | bytes 4194304 | tf_op jit(solution)/shard_map/sort_queries/pallas_call | solution.py:193
  68.4 0.0 collective-permute-done.2.refs_2_
  68.4 0.0 collective-permute-done.3.refs_3_
  68.4 49.1 %attend.3 = bf16[128,64,128]{2,1,0:T(8,128)(2,1)S(1)} custom-call(s32[3]{0:T(128)S(1)} %pad_add_fusion.facts_ref, f32[1,128,128]{2,1,0:T(8,128)S(1)} %get-tuple-element.65.column_ref, bf16[4,2048,128]{2,1,0:T(8,128)(2,1)S(1)} %sort_queries.3.q_ref, bf16[2048,128]{1,0:T(8,128)(2,1)} %get-tuple-element.66.refs_0_, ...), custom_call_target="tpu_custom_call" | custom-call | tf_op jit(solution)/shard_map/attend/pallas_call | solution.py:352
  117.5 43.1 %all_to_all.29 = bf16[128,64,128]{2,1,0:T(8,128)(2,1)S(1)} all-to-all(bf16[128,64,128]{2,1,0:T(8,128)(2,1)S(1)} %attend.3), channel_id=1, replica_groups=mesh['inst'=4,'seq'=32] {'inst','seq'}, dimensions={0} | all-to-all | bytes 4194304 | tf_op jit(solution)/shard_map/all_to_all | solution.py:403
  160.6 0.0 copy-start.3
  160.6 0.0 copy-start.4
  160.6 2.0 %unpack.3 = bf16[128,8192]{1,0:T(8,128)(2,1)} custom-call(bf16[128,128]{1,0:T(8,128)(2,1)S(1)} %get-tuple-element.63.refs_0_, bf16[2,2,2,8,2,64,128]{6,5,4,3,2,1,0:T(8,128)(2,1)S(1)} %bitcast.14), custom_call_target="tpu_custom_call" | custom-call | tf_op jit(solution)/shard_map/unpack/pallas_call | solution.py:391
  162.6 0.0 copy-done.3
  162.6 0.0 copy-done.4
  162.6 0.9 while.9
Async XLA Ops:
  0.0 63.6 %copy-start = (s32[4,2]{0,1:T(2,128)S(1)}, s32[4,2]{0,1:T(2,128)}, u32[]{:S(2)}) copy-start(s32[4,2]{0,1:T(2,128)} %param.13) | copy-start | bytes 100
  62.3 6.1 %collective-permute-start.2 = (bf16[2048,128]{1,0:T(8,128)(2,1)}, bf16[2048,128]{1,0:T(8,128)(2,1)}, u32[]{:S(2)}, u32[]{:S(2)}) collective-permute-start(bf16[2048,128]{1,0:T(8,128)(2,1)} %get-tuple-element.66.refs_0_), channel_id=1, source_target_pairs={{0,32},{32,0},{64,96},{96,64},{1,33},{33,1},{65,97},{97,65},{2,34}... | collective-permute-start | bytes 1572872 | tf_op jit(solution)/shard_map/ppermute | solution.py:419
  63.5 4.9 %collective-permute-start.3 = (bf16[128,2048]{1,0:T(8,128)(2,1)}, bf16[128,2048]{1,0:T(8,128)(2,1)}, u32[]{:S(2)}, u32[]{:S(2)}) collective-permute-start(bf16[128,2048]{1,0:T(8,128)(2,1)} %get-tuple-element.67.refs_1_), channel_id=1, source_target_pairs={{0,32},{32,0},{64,96},{96,64},{1,33},{33,1},{65,97},{97,65},{2,34}... | collective-permute-start | bytes 1572872 | tf_op jit(solution)/shard_map/ppermute | solution.py:419
  160.6 2.0 %copy-start.3 = (s32[64]{0:T(128)S(1)}, s32[64]{0:T(128)}, u32[]{:S(2)}) copy-start(s32[64]{0:T(128)} %param.11) | copy-start | bytes 772
  160.6 2.0 %copy-start.4 = (s32[64]{0:T(128)S(1)}, s32[64]{0:T(128)}, u32[]{:S(2)}) copy-start(s32[64]{0:T(128)} %param.12) | copy-start | bytes 772

commit v5 on v4

--- a/solution.py
+++ b/solution.py
@@ -253,6 +253,27 @@
         values = jnp.concatenate([values, ones], axis=0)
         return jnp.dot(values, weights.astype(BF16), preferred_element_type=F32)
 
+    def own_tile_weights():
+        scores = scores_of(tile, 1)
+        key_at = lax.broadcasted_iota(jnp.int32, (HEAD, HEAD), 0) * 2
+        query_at = lax.broadcasted_iota(jnp.int32, (HEAD, HEAD), 1) * 2
+        lines = []
+        for k in range(span // HEAD):
+            gap = query_at - key_at - (core if k < TILE // HEAD else 1 - core)
+            line = []
+            for c in range(columns // HEAD):
+                piece = scores[k * HEAD : (k + 1) * HEAD, c * HEAD : (c + 1) * HEAD]
+                ahead = k % (TILE // HEAD) - c % (TILE // HEAD)
+                if ahead > 0:
+                    line.append(jnp.zeros((HEAD, HEAD), BF16))
+                elif ahead < 0:
+                    line.append(jnp.exp2(piece).astype(BF16))
+                else:
+                    seen = gap + c // (2 * TILE // HEAD) >= 0
+                    line.append(jnp.where(seen, jnp.exp2(piece), 0.0).astype(BF16))
+            lines.append(jnp.concatenate(line, axis=1))
+        return jnp.concatenate(lines, axis=0)
+
     start = start_of(first)
     low = start // span
 
@@ -284,7 +305,7 @@
 
         @pl.when(jnp.logical_not(split))
         def _():
-            sum_ref[...] = mixed(tile, 1, jnp.exp2(allowed_scores(tile, False)))
+            sum_ref[...] = mixed(tile, 1, own_tile_weights())
 
         left = tile - low
         for wide in (1, 2, 4):

time: 164 us -> 160 us (0.976); the launches traced: 164 us -> 163 us
  blocking collectives: 99.1 us -> 89.9 us
  Pallas kernels: 61.8 us -> 70.5 us
    all_to_all x2, blocking collectives: 99.1 us -> 89.9 us  [exchange(): return lax.all_to_all(x, BOTH, split_axis=0, concat_axis=0, tiled=True)]
    pallas_call x1, Pallas kernels: 49.1 us -> 57.7 us  [attend(): pl.pallas_call(attend_kernel, in_specs=[NEAR] + [HERE] * 6, out_specs=HER...]
where the time goes in v5:
time: 160 us; the launch traced here: 163 us
  blocking collectives  89.9 us (56%)
  Pallas kernels  70.5 us (44%)
    all_to_all x2, blocking collectives, exchange(): return lax.all_to_all(x, BOTH, split_axis=0, concat_axis=0, tiled=True)  89.9 us
    pallas_call x1, Pallas kernels, attend(): pl.pallas_call(attend_kernel, in_specs=[NEAR] + [HERE] * 6, out_specs=HER...  57.7 us
    pallas_call x1, Pallas kernels, sort_queries(): pl.pallas_call(sort_queries_kernel, in_specs=[HERE] * len(rows), out_spec...  4.49 us
    pallas_call x1, Pallas kernels, sort_keys(): pl.pallas_call(functools.partial(sort_keys_kernel, rounds), in_specs=[HER...  3.31 us
  transfers between devices with their start and end apart: 2, of which 0 were waited for; matrix products, arithmetic and copies ran while one was open for 0% of the time, Pallas kernels for 3%

profile of v5, /device:TPU:1, one launch (start us, length us, event | category | flops | bytes accessed | tf_op | source)
XLA Modules:
  0.0 163.2 jit_solution(15210183621151035907)
XLA Ops:
  0.0 0.0 copy-start
  0.0 3.0 %pack.5 = (bf16[2,2,2,8,2,104,128]{6,5,4,3,2,1,0:T(8,128)(2,1)S(1)}, bf16[128,128]{1,0:T(8,128)(2,1)S(1)}) custom-call(s32[1]{0:T(128)} %bitcast.4.offset_ref, s32[1,64]{1,0:T(1,128)} %bitcast.16, s32[1,64]{1,0:T(1,128)} %bitcast.18, bf16[128,8192]{1,0:T(8,128)(2,1)} %q_ref.1, bf16[128,1024]{1,0:T(8,128)(2,1)} %k_ref.1, bf16[128,1024]{1,0:T(8,128)(2,1)} %v_ref.1), custom_call_target="tpu_custom_call" | custom-call | tf_op jit(solution)/shard_map/pack/pallas_call | solution.py:96
  3.0 56.0 %all_to_all.28.refs_0_ = bf16[128,104,128]{2,1,0:T(8,128)(2,1)S(1)} all-to-all(bf16[128,104,128]{2,1,0:T(8,128)(2,1)S(1)} %bitcast.15), channel_id=1, replica_groups=mesh['inst'=4,'seq'=32] {'inst','seq'}, dimensions={0} | all-to-all | bytes 6815744 | tf_op jit(solution)/shard_map/all_to_all | solution.py:424
  58.9 3.3 %sort_keys.3 = (bf16[2048,128]{1,0:T(8,128)(2,1)}, bf16[128,2048]{1,0:T(8,128)(2,1)}, f32[1,128,128]{2,1,0:T(8,128)S(1)}, s32[1]{0:T(128)}) custom-call(bf16[128,104,128]{2,1,0:T(8,128)(2,1)S(1)} %all_to_all.28.refs_0_), custom_call_target="tpu_custom_call" | custom-call | tf_op jit(solution)/shard_map/sort_keys/pallas_call | solution.py:166
  62.3 1.2 collective-permute-start.2
  63.5 0.1 collective-permute-start.3
  63.6 0.0 copy-done
  63.6 0.2 dynamic-slice_reduce_fusion
  63.8 0.1 pad_add_fusion.facts_ref
  63.9 4.5 %sort_queries.3.q_ref = bf16[4,2048,128]{2,1,0:T(8,128)(2,1)S(1)} custom-call(bf16[128,104,128]{2,1,0:T(8,128)(2,1)S(1)} %all_to_all.28.refs_0_), custom_call_target="tpu_custom_call" | custom-call | flops 4294967296 | bytes 4194304 | tf_op jit(solution)/shard_map/sort_queries/pallas_call | solution.py:193
  68.4 0.0 collective-permute-done.2.refs_2_
  68.4 0.0 collective-permute-done.3.refs_3_
  68.4 57.7 %attend.3 = bf16[128,64,128]{2,1,0:T(8,128)(2,1)S(1)} custom-call(s32[3]{0:T(128)S(1)} %pad_add_fusion.facts_ref, f32[1,128,128]{2,1,0:T(8,128)S(1)} %get-tuple-element.65.column_ref, bf16[4,2048,128]{2,1,0:T(8,128)(2,1)S(1)} %sort_queries.3.q_ref, bf16[2048,128]{1,0:T(8,128)(2,1)} %get-tuple-element.66.refs_0_, ...), custom_call_target="tpu_custom_call" | custom-call | tf_op jit(solution)/shard_map/attend/pallas_call | solution.py:373
  126.1 33.9 %all_to_all.29 = bf16[128,64,128]{2,1,0:T(8,128)(2,1)S(1)} all-to-all(bf16[128,64,128]{2,1,0:T(8,128)(2,1)S(1)} %attend.3), channel_id=1, replica_groups=mesh['inst'=4,'seq'=32] {'inst','seq'}, dimensions={0} | all-to-all | bytes 4194304 | tf_op jit(solution)/shard_map/all_to_all | solution.py:424
  160.1 0.0 copy-start.3
  160.1 0.0 copy-start.4
  160.1 2.0 %unpack.3 = bf16[128,8192]{1,0:T(8,128)(2,1)} custom-call(bf16[128,128]{1,0:T(8,128)(2,1)S(1)} %get-tuple-element.63.refs_0_, bf16[2,2,2,8,2,64,128]{6,5,4,3,2,1,0:T(8,128)(2,1)S(1)} %bitcast.14), custom_call_target="tpu_custom_call" | custom-call | tf_op jit(solution)/shard_map/unpack/pallas_call | solution.py:412
  162.1 0.0 copy-done.3
  162.1 0.0 copy-done.4
  162.1 0.9 while.9
Async XLA Ops:
  0.0 63.6 %copy-start = (s32[4,2]{0,1:T(2,128)S(1)}, s32[4,2]{0,1:T(2,128)}, u32[]{:S(2)}) copy-start(s32[4,2]{0,1:T(2,128)} %param.13) | copy-start | bytes 100
  62.3 6.1 %collective-permute-start.2 = (bf16[2048,128]{1,0:T(8,128)(2,1)}, bf16[2048,128]{1,0:T(8,128)(2,1)}, u32[]{:S(2)}, u32[]{:S(2)}) collective-permute-start(bf16[2048,128]{1,0:T(8,128)(2,1)} %get-tuple-element.66.refs_0_), channel_id=1, source_target_pairs={{0,32},{32,0},{64,96},{96,64},{1,33},{33,1},{65,97},{97,65},{2,34}... | collective-permute-start | bytes 1572872 | tf_op jit(solution)/shard_map/ppermute | solution.py:440
  63.5 4.9 %collective-permute-start.3 = (bf16[128,2048]{1,0:T(8,128)(2,1)}, bf16[128,2048]{1,0:T(8,128)(2,1)}, u32[]{:S(2)}, u32[]{:S(2)}) collective-permute-start(bf16[128,2048]{1,0:T(8,128)(2,1)} %get-tuple-element.67.refs_1_), channel_id=1, source_target_pairs={{0,32},{32,0},{64,96},{96,64},{1,33},{33,1},{65,97},{97,65},{2,34}... | collective-permute-start | bytes 1572872 | tf_op jit(solution)/shard_map/ppermute | solution.py:440
  160.1 2.0 %copy-start.3 = (s32[64]{0:T(128)S(1)}, s32[64]{0:T(128)}, u32[]{:S(2)}) copy-start(s32[64]{0:T(128)} %param.11) | copy-start | bytes 772
  160.1 2.0 %copy-start.4 = (s32[64]{0:T(128)S(1)}, s32[64]{0:T(128)}, u32[]{:S(2)}) copy-start(s32[64]{0:T(128)} %param.12) | copy-start | bytes 772
